TPU v7x, 512 devices: a whole 4x8x8 slice. The times are simulated.
512 devices in a mesh: row: 32 (over z_lo, y), col: 16 (over x, z_hi, core).
Axes of the slice: x: 4, y: 8, z: 8 (z_hi: 2, z_lo: 4; z = z_hi * 4 + z_lo), core: 2. Of those that a mesh axis runs over, the one named last changes fastest.
Arguments:
- a_vals: bfloat16 [32, 16, 4, 5, 9216], P('row', 'col'), may hold values from -1.5 to 1.5
- a_cols: int32 [32, 16, 4, 5], P('row', 'col'), may hold values from 0 to 7, as said below
- a_count: int32 [32, 16, 4], P('row', 'col'), may hold values from 1 to 5, as said below
- b_vals: bfloat16 [32, 16, 8, 2, 9216], P('row', 'col'), may hold values from -1.5 to 1.5, as said below
- b_cols: int32 [32, 16, 8, 2], P('row', 'col'), may hold values from 0 to 7, as said below
- b_count: int32 [32, 16, 8], P('row', 'col'), may hold values from 0 to 2, as said below
Outputs:
- next_sign: bfloat16 [12288, 12288], P('row', 'col')
Inputs may be any that keep to these rules, and one draw needn't show every extreme that they name: `a_cols`: the block columns within one block row of a tile are distinct. `a_count`: in every grid row one tile holds 5 blocks in each of its block rows. `b_vals`: entry [u, c] equals entry [u mod Q, c], Q the number of grid columns. `b_cols`: the block columns within one block row of a tile are distinct; entry [u, c] equals entry [u mod Q, c], Q the number of grid columns. `b_count`: in every grid column one tile holds 2 blocks in each of its block rows; entry [u, c] equals entry [u mod Q, c], Q the number of grid columns.
All inputs are finite; a program needn't handle non-finite values.
Results may differ from a plain program's by a relative error of at most 0.001.
Values may be sent and summed in bfloat16 or wider, within the bound.
A program may use at most 64 MiB of HBM per device.

v0:
```python
import jax
import jax.numpy as jnp
from jax import lax
from jax.sharding import PartitionSpec as P

BLOCK = 96


def passed_along(shard, axis, by):
    count = lax.axis_size(axis)
    return lax.ppermute(shard, axis, [(i, (i + by) % count) for i in range(count)])


def dense_panel(b_blocks, b_where, b_number):
    block_cols, b_slots = b_where.shape
    b_live = jnp.arange(b_slots, dtype=jnp.int32)[None, :] < b_number[:, None]
    placing = (
        (b_where[..., None] == jnp.arange(block_cols, dtype=jnp.int32)) & b_live[..., None]
    ).astype(jnp.bfloat16)
    blocks = b_blocks.reshape(block_cols, b_slots, BLOCK, BLOCK)
    panel = jnp.einsum("kqj,kqzy->kzjy", placing, blocks, preferred_element_type=jnp.float32)
    return panel.astype(jnp.bfloat16).reshape(block_cols, BLOCK, block_cols * BLOCK)


def tile_term(a_blocks, a_where, a_number, b_blocks, b_where, b_number):
    block_rows, a_slots = a_where.shape
    a_live = (jnp.arange(a_slots, dtype=jnp.int32)[None, :] < a_number[:, None]).astype(
        jnp.bfloat16
    )
    panel = dense_panel(b_blocks, b_where, b_number)
    picked_rows = panel[a_where]
    blocks = a_blocks.reshape(block_rows, a_slots, BLOCK, BLOCK) * a_live[:, :, None, None]
    return jnp.einsum("ipxk,ipkn->ixn", blocks, picked_rows, preferred_element_type=jnp.float32)


def own_dense(a_blocks, a_where, a_number, block_cols):
    block_rows, a_slots = a_where.shape
    a_live = jnp.arange(a_slots, dtype=jnp.int32)[None, :] < a_number[:, None]
    placing = (
        (a_where[..., None] == jnp.arange(block_cols, dtype=jnp.int32)) & a_live[..., None]
    ).astype(jnp.float32)
    blocks = a_blocks.reshape(block_rows, a_slots, BLOCK, BLOCK).astype(jnp.float32)
    placed = jnp.einsum("ipj,ipxy->ixjy", placing, blocks, precision=lax.Precision.HIGHEST)
    return placed.reshape(block_rows, BLOCK, block_cols * BLOCK)


def unwrap(pieces):
    return tuple((piece[0, 0] for piece in pieces))


def shards(a_vals, a_cols, a_count, b_vals, b_cols, b_count):
    loop_length = lax.axis_size("col")
    row_place = lax.axis_index("row")
    block_rows = a_cols.shape[2]
    block_cols = b_cols.shape[2]
    a_start = (a_vals, a_cols, a_count)
    b_start = (b_vals, b_cols, b_count)
    own_step = -row_place % loop_length

    def current_a(a_now):
        return unwrap(a_now)

    def current_b(b_now):
        return unwrap(b_now)

    def advance(shift_step, loop_state):
        summed, a_now, own_tile, b_now = loop_state
        summed = summed + tile_term(*current_a(a_now), *current_b(b_now))
        b_now = passed_along((b_now[0], b_now[1], b_now[2]), "row", -1)
        own_tile = tuple(
            (
                jnp.where(shift_step == own_step, arrived, stored)
                for arrived, stored in zip(a_now, own_tile)
            )
        )
        a_now = passed_along((a_now[0], a_now[1], a_now[2]), "col", -1)
        return (summed, a_now, own_tile, b_now)

    zero_sum = jnp.zeros((block_rows, BLOCK, block_cols * BLOCK), jnp.float32)
    summed, a_now, own_tile, b_now = lax.fori_loop(
        0, loop_length - 1, advance, (zero_sum, a_start, a_start, b_start)
    )
    last_step = loop_length - 1
    summed = summed + tile_term(*current_a(a_now), *current_b(b_now))
    own_pieces = unwrap(
        tuple(
            (
                jnp.where(own_step == last_step, arrived, stored)
                for arrived, stored in zip(a_now, own_tile)
            )
        )
    )
    own_part = own_dense(*own_pieces, block_cols)
    result = 1.5 * own_part - 0.5 * summed
    return result.astype(jnp.bfloat16).reshape(block_rows * BLOCK, block_cols * BLOCK)


def solution(mesh):
    in_specs = (
        P("row", "col", None, None, None),
        P("row", "col", None, None),
        P("row", "col", None),
        P("row", "col", None, None, None),
        P("row", "col", None, None),
        P("row", "col", None),
    )
    out_specs = P("row", "col")
    return jax.shard_map(shards, mesh=mesh, in_specs=in_specs, out_specs=out_specs, check_vma=False)
```

profile of v0, /device:TPU:56, one launch (start us, length us, event | category | flops | bytes accessed | tf_op | source)
XLA Modules:
  0.0 582.7 jit_solution(12340975764729061134)
XLA Ops:
  7.0 559.1 %while.32 = (s32[]{:T(128)}, f32[4,96,768]{2,1,0:T(8,128)}, bf16[1,1,4,5,9216]{4,2,3,1,0:T(4,128)(2,1)}, s32[1,1,4,5]{3,2,1,0:T(4,128)S(1)}, s32[1,1,4]{2,1,0:T(...) while((s32[]{:T(128)}, f32[4,96,768]{2,1,0:T(8,128)}, ...), condition=%wide.region_1.2_spmd.clone, body=%wide.region_0.1_spmd.clone.sunk | while | flops 287024544 | bytes 32742384 | solution.py:80
  8.0 12.5 %collective-permute-start = (bf16[1,1,4,5,9216]{4,2,3,1,0:T(4,128)(2,1)S(1)}, bf16[1,1,4,5,9216]{4,2,3,1,0:T(4,128)(2,1)}, u32[]{:S(2)}, u32[]{:S(2)}) collective-permute-start(bf16[1,1,4,5,9216]{4,2,3,1,0:T(4,128)(2,1)S(1)} %copy.71), channel_id=1, source_target_pairs={{0,15},{1,0},{2,1},{3,2},{4,3},{5,4},{6,5},{7,6},{8,7},{9,8},{10,9... | collective-permute-start | bytes 1105928 | tf_op jit(solution)/shard_map/while/body/eval_jaxpr/ppermute | solution.py:11
  54.3 7.6 %collective-permute-start.1 = (s32[1,1,4,5]{3,2,1,0:T(4,128)S(1)}, s32[1,1,4,5]{3,2,1,0:T(4,128)S(1)}, u32[]{:S(2)}, u32[]{:S(2)}) collective-permute-start(s32[1,1,4,5]{3,2,1,0:T(4,128)S(1)} %copy.72), channel_id=1, source_target_pairs={{0,15},{1,0},{2,1},{3,2},{4,3},{5,4},{6,5},{7,6},{8,7},{9,8},{10,9... | collective-permute-start | bytes 248 | tf_op jit(solution)/shard_map/while/body/eval_jaxpr/ppermute | solution.py:11
  81.9 5.5 collective-permute-done.5
  93.0 6.2 %collective-permute-start.2 = (s32[1,1,4]{2,1,0:T(1,128)S(1)}, s32[1,1,4]{2,1,0:T(1,128)S(1)}, u32[]{:S(2)}, u32[]{:S(2)}) collective-permute-start(s32[1,1,4]{2,1,0:T(1,128)S(1)} %copy.73), channel_id=1, source_target_pairs={{0,15},{1,0},{2,1},{3,2},{4,3},{5,4},{6,5},{7,6},{8,7},{9,8},{10,9... | collective-permute-start | bytes 56 | tf_op jit(solution)/shard_map/while/body/eval_jaxpr/ppermute | solution.py:11
  135.5 5.1 collective-permute-start.4
  160.4 4.9 collective-permute-start
  193.1 4.6 collective-permute-done.5
  200.7 8.5 %collective-permute-start.1 = (s32[1,1,4,5]{3,2,1,0:T(4,128)S(1)}, s32[1,1,4,5]{3,2,1,0:T(4,128)S(1)}, u32[]{:S(2)}, u32[]{:S(2)}) collective-permute-start(s32[1,1,4,5]{3,2,1,0:T(4,128)S(1)} %copy.72), channel_id=1, source_target_pairs={{0,15},{1,0},{2,1},{3,2},{4,3},{5,4},{6,5},{7,6},{8,7},{9,8},{10,9... | collective-permute-start | bytes 248 | tf_op jit(solution)/shard_map/while/body/eval_jaxpr/ppermute | solution.py:11
  232.3 4.8 collective-permute-done.5
  243.7 4.9 collective-permute-start.2
  269.6 4.3 collective-permute-done.5
  303.3 5.2 collective-permute-done.5
  309.5 4.7 collective-permute-start
  340.5 4.6 collective-permute-done.5
  348.0 6.3 %collective-permute-start.1 = (s32[1,1,4,5]{3,2,1,0:T(4,128)S(1)}, s32[1,1,4,5]{3,2,1,0:T(4,128)S(1)}, u32[]{:S(2)}, u32[]{:S(2)}) collective-permute-start(s32[1,1,4,5]{3,2,1,0:T(4,128)S(1)} %copy.72), channel_id=1, source_target_pairs={{0,15},{1,0},{2,1},{3,2},{4,3},{5,4},{6,5},{7,6},{8,7},{9,8},{10,9... | collective-permute-start | bytes 248 | tf_op jit(solution)/shard_map/while/body/eval_jaxpr/ppermute | solution.py:11
  387.8 6.8 %collective-permute-start.2 = (s32[1,1,4]{2,1,0:T(1,128)S(1)}, s32[1,1,4]{2,1,0:T(1,128)S(1)}, u32[]{:S(2)}, u32[]{:S(2)}) collective-permute-start(s32[1,1,4]{2,1,0:T(1,128)S(1)} %copy.73), channel_id=1, source_target_pairs={{0,15},{1,0},{2,1},{3,2},{4,3},{5,4},{6,5},{7,6},{8,7},{9,8},{10,9... | collective-permute-start | bytes 56 | tf_op jit(solution)/shard_map/while/body/eval_jaxpr/ppermute | solution.py:11
  415.7 5.3 collective-permute-done.5
  450.7 4.7 collective-permute-done.5
  456.5 4.8 collective-permute-start
  494.5 6.3 %collective-permute-start.1 = (s32[1,1,4,5]{3,2,1,0:T(4,128)S(1)}, s32[1,1,4,5]{3,2,1,0:T(4,128)S(1)}, u32[]{:S(2)}, u32[]{:S(2)}) collective-permute-start(s32[1,1,4,5]{3,2,1,0:T(4,128)S(1)} %copy.72), channel_id=1, source_target_pairs={{0,15},{1,0},{2,1},{3,2},{4,3},{5,4},{6,5},{7,6},{8,7},{9,8},{10,9... | collective-permute-start | bytes 248 | tf_op jit(solution)/shard_map/while/body/eval_jaxpr/ppermute | solution.py:11
  524.7 4.9 collective-permute-done.5
  532.5 4.4 collective-permute-start.1
  561.5 4.6 collective-permute-done.5
  (659 shorter events, 448.0 us)
Async XLA Ops:
  8.0 43.3 %collective-permute-start = (bf16[1,1,4,5,9216]{4,2,3,1,0:T(4,128)(2,1)S(1)}, bf16[1,1,4,5,9216]{4,2,3,1,0:T(4,128)(2,1)}, u32[]{:S(2)}, u32[]{:S(2)}) collective-permute-start(bf16[1,1,4,5,9216]{4,2,3,1,0:T(4,128)(2,1)S(1)} %copy.71), channel_id=1, source_target_pairs={{0,15},{1,0},{2,1},{3,2},{4,3},{5,4},{6,5},{7,6},{8,7},{9,8},{10,9... | collective-permute-start | bytes 1105928 | tf_op jit(solution)/shard_map/while/body/eval_jaxpr/ppermute | solution.py:11
  52.3 35.1 %collective-permute-start = (bf16[1,1,4,5,9216]{4,2,3,1,0:T(4,128)(2,1)S(1)}, bf16[1,1,4,5,9216]{4,2,3,1,0:T(4,128)(2,1)}, u32[]{:S(2)}, u32[]{:S(2)}) collective-permute-start(bf16[1,1,4,5,9216]{4,2,3,1,0:T(4,128)(2,1)S(1)} %copy.71), channel_id=1, source_target_pairs={{0,15},{1,0},{2,1},{3,2},{4,3},{5,4},{6,5},{7,6},{8,7},{9,8},{10,9... | collective-permute-start | bytes 1105928 | tf_op jit(solution)/shard_map/while/body/eval_jaxpr/ppermute | solution.py:11
  54.3 33.2 %collective-permute-start.1 = (s32[1,1,4,5]{3,2,1,0:T(4,128)S(1)}, s32[1,1,4,5]{3,2,1,0:T(4,128)S(1)}, u32[]{:S(2)}, u32[]{:S(2)}) collective-permute-start(s32[1,1,4,5]{3,2,1,0:T(4,128)S(1)} %copy.72), channel_id=1, source_target_pairs={{0,15},{1,0},{2,1},{3,2},{4,3},{5,4},{6,5},{7,6},{8,7},{9,8},{10,9... | collective-permute-start | bytes 248 | tf_op jit(solution)/shard_map/while/body/eval_jaxpr/ppermute | solution.py:11
  88.5 34.7 %collective-permute-start = (bf16[1,1,4,5,9216]{4,2,3,1,0:T(4,128)(2,1)S(1)}, bf16[1,1,4,5,9216]{4,2,3,1,0:T(4,128)(2,1)}, u32[]{:S(2)}, u32[]{:S(2)}) collective-permute-start(bf16[1,1,4,5,9216]{4,2,3,1,0:T(4,128)(2,1)S(1)} %copy.71), channel_id=1, source_target_pairs={{0,15},{1,0},{2,1},{3,2},{4,3},{5,4},{6,5},{7,6},{8,7},{9,8},{10,9... | collective-permute-start | bytes 1105928 | tf_op jit(solution)/shard_map/while/body/eval_jaxpr/ppermute | solution.py:11
  90.4 32.7 %collective-permute-start.1 = (s32[1,1,4,5]{3,2,1,0:T(4,128)S(1)}, s32[1,1,4,5]{3,2,1,0:T(4,128)S(1)}, u32[]{:S(2)}, u32[]{:S(2)}) collective-permute-start(s32[1,1,4,5]{3,2,1,0:T(4,128)S(1)} %copy.72), channel_id=1, source_target_pairs={{0,15},{1,0},{2,1},{3,2},{4,3},{5,4},{6,5},{7,6},{8,7},{9,8},{10,9... | collective-permute-start | bytes 248 | tf_op jit(solution)/shard_map/while/body/eval_jaxpr/ppermute | solution.py:11
  124.1 35.2 %collective-permute-start = (bf16[1,1,4,5,9216]{4,2,3,1,0:T(4,128)(2,1)S(1)}, bf16[1,1,4,5,9216]{4,2,3,1,0:T(4,128)(2,1)}, u32[]{:S(2)}, u32[]{:S(2)}) collective-permute-start(bf16[1,1,4,5,9216]{4,2,3,1,0:T(4,128)(2,1)S(1)} %copy.71), channel_id=1, source_target_pairs={{0,15},{1,0},{2,1},{3,2},{4,3},{5,4},{6,5},{7,6},{8,7},{9,8},{10,9... | collective-permute-start | bytes 1105928 | tf_op jit(solution)/shard_map/while/body/eval_jaxpr/ppermute | solution.py:11
  126.1 33.3 %collective-permute-start.1 = (s32[1,1,4,5]{3,2,1,0:T(4,128)S(1)}, s32[1,1,4,5]{3,2,1,0:T(4,128)S(1)}, u32[]{:S(2)}, u32[]{:S(2)}) collective-permute-start(s32[1,1,4,5]{3,2,1,0:T(4,128)S(1)} %copy.72), channel_id=1, source_target_pairs={{0,15},{1,0},{2,1},{3,2},{4,3},{5,4},{6,5},{7,6},{8,7},{9,8},{10,9... | collective-permute-start | bytes 248 | tf_op jit(solution)/shard_map/while/body/eval_jaxpr/ppermute | solution.py:11
  160.4 37.3 %collective-permute-start = (bf16[1,1,4,5,9216]{4,2,3,1,0:T(4,128)(2,1)S(1)}, bf16[1,1,4,5,9216]{4,2,3,1,0:T(4,128)(2,1)}, u32[]{:S(2)}, u32[]{:S(2)}) collective-permute-start(bf16[1,1,4,5,9216]{4,2,3,1,0:T(4,128)(2,1)S(1)} %copy.71), channel_id=1, source_target_pairs={{0,15},{1,0},{2,1},{3,2},{4,3},{5,4},{6,5},{7,6},{8,7},{9,8},{10,9... | collective-permute-start | bytes 1105928 | tf_op jit(solution)/shard_map/while/body/eval_jaxpr/ppermute | solution.py:11
  198.7 38.3 %collective-permute-start = (bf16[1,1,4,5,9216]{4,2,3,1,0:T(4,128)(2,1)S(1)}, bf16[1,1,4,5,9216]{4,2,3,1,0:T(4,128)(2,1)}, u32[]{:S(2)}, u32[]{:S(2)}) collective-permute-start(bf16[1,1,4,5,9216]{4,2,3,1,0:T(4,128)(2,1)S(1)} %copy.71), channel_id=1, source_target_pairs={{0,15},{1,0},{2,1},{3,2},{4,3},{5,4},{6,5},{7,6},{8,7},{9,8},{10,9... | collective-permute-start | bytes 1105928 | tf_op jit(solution)/shard_map/while/body/eval_jaxpr/ppermute | solution.py:11
  200.7 36.4 %collective-permute-start.1 = (s32[1,1,4,5]{3,2,1,0:T(4,128)S(1)}, s32[1,1,4,5]{3,2,1,0:T(4,128)S(1)}, u32[]{:S(2)}, u32[]{:S(2)}) collective-permute-start(s32[1,1,4,5]{3,2,1,0:T(4,128)S(1)} %copy.72), channel_id=1, source_target_pairs={{0,15},{1,0},{2,1},{3,2},{4,3},{5,4},{6,5},{7,6},{8,7},{9,8},{10,9... | collective-permute-start | bytes 248 | tf_op jit(solution)/shard_map/while/body/eval_jaxpr/ppermute | solution.py:11
  238.1 35.9 %collective-permute-start = (bf16[1,1,4,5,9216]{4,2,3,1,0:T(4,128)(2,1)S(1)}, bf16[1,1,4,5,9216]{4,2,3,1,0:T(4,128)(2,1)}, u32[]{:S(2)}, u32[]{:S(2)}) collective-permute-start(bf16[1,1,4,5,9216]{4,2,3,1,0:T(4,128)(2,1)S(1)} %copy.71), channel_id=1, source_target_pairs={{0,15},{1,0},{2,1},{3,2},{4,3},{5,4},{6,5},{7,6},{8,7},{9,8},{10,9... | collective-permute-start | bytes 1105928 | tf_op jit(solution)/shard_map/while/body/eval_jaxpr/ppermute | solution.py:11
  240.0 33.9 %collective-permute-start.1 = (s32[1,1,4,5]{3,2,1,0:T(4,128)S(1)}, s32[1,1,4,5]{3,2,1,0:T(4,128)S(1)}, u32[]{:S(2)}, u32[]{:S(2)}) collective-permute-start(s32[1,1,4,5]{3,2,1,0:T(4,128)S(1)} %copy.72), channel_id=1, source_target_pairs={{0,15},{1,0},{2,1},{3,2},{4,3},{5,4},{6,5},{7,6},{8,7},{9,8},{10,9... | collective-permute-start | bytes 248 | tf_op jit(solution)/shard_map/while/body/eval_jaxpr/ppermute | solution.py:11
  275.0 33.4 %collective-permute-start = (bf16[1,1,4,5,9216]{4,2,3,1,0:T(4,128)(2,1)S(1)}, bf16[1,1,4,5,9216]{4,2,3,1,0:T(4,128)(2,1)}, u32[]{:S(2)}, u32[]{:S(2)}) collective-permute-start(bf16[1,1,4,5,9216]{4,2,3,1,0:T(4,128)(2,1)S(1)} %copy.71), channel_id=1, source_target_pairs={{0,15},{1,0},{2,1},{3,2},{4,3},{5,4},{6,5},{7,6},{8,7},{9,8},{10,9... | collective-permute-start | bytes 1105928 | tf_op jit(solution)/shard_map/while/body/eval_jaxpr/ppermute | solution.py:11
  309.5 35.6 %collective-permute-start = (bf16[1,1,4,5,9216]{4,2,3,1,0:T(4,128)(2,1)S(1)}, bf16[1,1,4,5,9216]{4,2,3,1,0:T(4,128)(2,1)}, u32[]{:S(2)}, u32[]{:S(2)}) collective-permute-start(bf16[1,1,4,5,9216]{4,2,3,1,0:T(4,128)(2,1)S(1)} %copy.71), channel_id=1, source_target_pairs={{0,15},{1,0},{2,1},{3,2},{4,3},{5,4},{6,5},{7,6},{8,7},{9,8},{10,9... | collective-permute-start | bytes 1105928 | tf_op jit(solution)/shard_map/while/body/eval_jaxpr/ppermute | solution.py:11
  346.1 35.1 %collective-permute-start = (bf16[1,1,4,5,9216]{4,2,3,1,0:T(4,128)(2,1)S(1)}, bf16[1,1,4,5,9216]{4,2,3,1,0:T(4,128)(2,1)}, u32[]{:S(2)}, u32[]{:S(2)}) collective-permute-start(bf16[1,1,4,5,9216]{4,2,3,1,0:T(4,128)(2,1)S(1)} %copy.71), channel_id=1, source_target_pairs={{0,15},{1,0},{2,1},{3,2},{4,3},{5,4},{6,5},{7,6},{8,7},{9,8},{10,9... | collective-permute-start | bytes 1105928 | tf_op jit(solution)/shard_map/while/body/eval_jaxpr/ppermute | solution.py:11
  348.0 33.2 %collective-permute-start.1 = (s32[1,1,4,5]{3,2,1,0:T(4,128)S(1)}, s32[1,1,4,5]{3,2,1,0:T(4,128)S(1)}, u32[]{:S(2)}, u32[]{:S(2)}) collective-permute-start(s32[1,1,4,5]{3,2,1,0:T(4,128)S(1)} %copy.72), channel_id=1, source_target_pairs={{0,15},{1,0},{2,1},{3,2},{4,3},{5,4},{6,5},{7,6},{8,7},{9,8},{10,9... | collective-permute-start | bytes 248 | tf_op jit(solution)/shard_map/while/body/eval_jaxpr/ppermute | solution.py:11
  382.3 38.8 %collective-permute-start = (bf16[1,1,4,5,9216]{4,2,3,1,0:T(4,128)(2,1)S(1)}, bf16[1,1,4,5,9216]{4,2,3,1,0:T(4,128)(2,1)}, u32[]{:S(2)}, u32[]{:S(2)}) collective-permute-start(bf16[1,1,4,5,9216]{4,2,3,1,0:T(4,128)(2,1)S(1)} %copy.71), channel_id=1, source_target_pairs={{0,15},{1,0},{2,1},{3,2},{4,3},{5,4},{6,5},{7,6},{8,7},{9,8},{10,9... | collective-permute-start | bytes 1105928 | tf_op jit(solution)/shard_map/while/body/eval_jaxpr/ppermute | solution.py:11
  384.2 36.8 %collective-permute-start.1 = (s32[1,1,4,5]{3,2,1,0:T(4,128)S(1)}, s32[1,1,4,5]{3,2,1,0:T(4,128)S(1)}, u32[]{:S(2)}, u32[]{:S(2)}) collective-permute-start(s32[1,1,4,5]{3,2,1,0:T(4,128)S(1)} %copy.72), channel_id=1, source_target_pairs={{0,15},{1,0},{2,1},{3,2},{4,3},{5,4},{6,5},{7,6},{8,7},{9,8},{10,9... | collective-permute-start | bytes 248 | tf_op jit(solution)/shard_map/while/body/eval_jaxpr/ppermute | solution.py:11
  422.1 33.5 %collective-permute-start = (bf16[1,1,4,5,9216]{4,2,3,1,0:T(4,128)(2,1)S(1)}, bf16[1,1,4,5,9216]{4,2,3,1,0:T(4,128)(2,1)}, u32[]{:S(2)}, u32[]{:S(2)}) collective-permute-start(bf16[1,1,4,5,9216]{4,2,3,1,0:T(4,128)(2,1)S(1)} %copy.71), channel_id=1, source_target_pairs={{0,15},{1,0},{2,1},{3,2},{4,3},{5,4},{6,5},{7,6},{8,7},{9,8},{10,9... | collective-permute-start | bytes 1105928 | tf_op jit(solution)/shard_map/while/body/eval_jaxpr/ppermute | solution.py:11
  456.5 34.8 %collective-permute-start = (bf16[1,1,4,5,9216]{4,2,3,1,0:T(4,128)(2,1)S(1)}, bf16[1,1,4,5,9216]{4,2,3,1,0:T(4,128)(2,1)}, u32[]{:S(2)}, u32[]{:S(2)}) collective-permute-start(bf16[1,1,4,5,9216]{4,2,3,1,0:T(4,128)(2,1)S(1)} %copy.71), channel_id=1, source_target_pairs={{0,15},{1,0},{2,1},{3,2},{4,3},{5,4},{6,5},{7,6},{8,7},{9,8},{10,9... | collective-permute-start | bytes 1105928 | tf_op jit(solution)/shard_map/while/body/eval_jaxpr/ppermute | solution.py:11
  492.3 37.2 %collective-permute-start = (bf16[1,1,4,5,9216]{4,2,3,1,0:T(4,128)(2,1)S(1)}, bf16[1,1,4,5,9216]{4,2,3,1,0:T(4,128)(2,1)}, u32[]{:S(2)}, u32[]{:S(2)}) collective-permute-start(bf16[1,1,4,5,9216]{4,2,3,1,0:T(4,128)(2,1)S(1)} %copy.71), channel_id=1, source_target_pairs={{0,15},{1,0},{2,1},{3,2},{4,3},{5,4},{6,5},{7,6},{8,7},{9,8},{10,9... | collective-permute-start | bytes 1105928 | tf_op jit(solution)/shard_map/while/body/eval_jaxpr/ppermute | solution.py:11
  494.5 35.1 %collective-permute-start.1 = (s32[1,1,4,5]{3,2,1,0:T(4,128)S(1)}, s32[1,1,4,5]{3,2,1,0:T(4,128)S(1)}, u32[]{:S(2)}, u32[]{:S(2)}) collective-permute-start(s32[1,1,4,5]{3,2,1,0:T(4,128)S(1)} %copy.72), channel_id=1, source_target_pairs={{0,15},{1,0},{2,1},{3,2},{4,3},{5,4},{6,5},{7,6},{8,7},{9,8},{10,9... | collective-permute-start | bytes 248 | tf_op jit(solution)/shard_map/while/body/eval_jaxpr/ppermute | solution.py:11
  530.5 35.5 %collective-permute-start = (bf16[1,1,4,5,9216]{4,2,3,1,0:T(4,128)(2,1)S(1)}, bf16[1,1,4,5,9216]{4,2,3,1,0:T(4,128)(2,1)}, u32[]{:S(2)}, u32[]{:S(2)}) collective-permute-start(bf16[1,1,4,5,9216]{4,2,3,1,0:T(4,128)(2,1)S(1)} %copy.71), channel_id=1, source_target_pairs={{0,15},{1,0},{2,1},{3,2},{4,3},{5,4},{6,5},{7,6},{8,7},{9,8},{10,9... | collective-permute-start | bytes 1105928 | tf_op jit(solution)/shard_map/while/body/eval_jaxpr/ppermute | solution.py:11
  532.5 33.6 %collective-permute-start.1 = (s32[1,1,4,5]{3,2,1,0:T(4,128)S(1)}, s32[1,1,4,5]{3,2,1,0:T(4,128)S(1)}, u32[]{:S(2)}, u32[]{:S(2)}) collective-permute-start(s32[1,1,4,5]{3,2,1,0:T(4,128)S(1)} %copy.72), channel_id=1, source_target_pairs={{0,15},{1,0},{2,1},{3,2},{4,3},{5,4},{6,5},{7,6},{8,7},{9,8},{10,9... | collective-permute-start | bytes 248 | tf_op jit(solution)/shard_map/while/body/eval_jaxpr/ppermute | solution.py:11
  (146 other events, 1643.4 us)
where the time goes:
time: 592 us; the launch traced here: 583 us
  starting transfers between devices  294 us (50%)
  local copies, waits for them, and re-layouts  128 us (22%)
  waiting for transfers between devices  67.1 us (11%)
  matrix products  58.9 us (10%)
  other arithmetic  31 us (5%)
    ppermute x90, starting transfers between devices, passed_along(): lax.ppermute(shard, axis, [(i, (i + by) % count) for i in range(count)])  294 us
    ppermute x90, waiting for transfers between devices, passed_along(): lax.ppermute(shard, axis, [(i, (i + by) % count) for i in range(count)])  67.1 us
    dot_general x16, matrix products, tile_term(): jnp.einsum('ipxk,ipkn->ixn', blocks, picked_rows, preferred_element_type=...  44.5 us
    gather x16, local copies, waits for them, and re-layouts, tile_term(): picked_rows = panel[a_where]  39.9 us
    while x240, local copies, waits for them, and re-layouts  29.8 us
    select_n x45, other arithmetic, advance(): jnp.where(shift_step == own_step, arrived, stored)  28.3 us
    reshape x16, local copies, waits for them, and re-layouts, dense_panel(): panel.astype(jnp.bfloat16).reshape(block_cols, BLOCK, block_cols * BLOCK)  22.8 us
    squeeze x15, local copies, waits for them, and re-layouts, tile_term(): a_blocks.reshape(block_rows, a_slots, BLOCK, BLOCK)  17.7 us
  transfers between devices with their start and end apart: 90, of which 15 were waited for; matrix products, arithmetic and copies ran while one was open for 31% of the time, Pallas kernels for 0%

commit v1 on v0

v1 whole, which is shorter than its diff:
```python
import functools

import jax
import jax.numpy as jnp
from jax import lax
from jax.experimental import pallas as pl
from jax.experimental.pallas import tpu as pltpu
from jax.sharding import PartitionSpec as P

BLOCK = 96
LANES = 128
ROWS = 4
SLOTS_X = 5
COLS = 8
SLOTS_S = 2
WIDE_X = ROWS * BLOCK // LANES
WIDE_S = COLS * BLOCK // LANES
DATA_X = WIDE_X * SLOTS_X * BLOCK
DATA_S = WIDE_S * SLOTS_S * BLOCK
META = 16
WIRE_X = DATA_X + META
WIRE_S = DATA_S + META
HALF_S = 592
MESH = pl.DeviceIdType.MESH
NEAR = (0, 1, -1, 2, -2, 3, -3, 4)
AROUND = (0, 1, 3, 2)


def s_slot(other, dy):
    return 8 * other + NEAR.index(4 if dy == -4 else dy)


def x_slot(other, dx, sibling):
    return 8 * other + 2 * AROUND.index(dx % 4) + sibling


def nt(left, right):
    return lax.dot_general(
        left, right, (((1,), (1,)), ((), ())), preferred_element_type=jnp.float32
    )


def kernel(
    a_cols, a_count, b_cols, b_count, x_in, s_in, out_ref,
    x_tiles, s_tiles, x_dense, s_dense, total, meta, x_recv, s_recv, sent,
):
    row, col = lax.axis_index("row"), lax.axis_index("col")
    y, z_lo = row % 8, row // 8
    core, z_hi, x = col % 2, (col // 2) % 2, col // 4
    parity = z_lo % 2

    def at(x_at, y_at, z_lo_at, z_hi_at, core_at):
        return (z_lo_at * 8 + y_at, (x_at * 2 + z_hi_at) * 2 + core_at)

    def along_x(d):
        return at((x + d + 4) % 4, y, z_lo, z_hi, core)

    def along_y(d):
        return at(x, (y + d + 8) % 8, z_lo, z_hi, core)

    pair_chip = at(x, y, z_lo + 1 - 2 * parity, z_hi, core)
    far_chip = at(x, y, z_lo, 1 - z_hi, core)
    sibling = at(x, y, z_lo, z_hi, 1 - core)
    partners = (
        along_x(1), along_x(-1), along_x(2), along_y(1), along_y(-1), pair_chip, far_chip, sibling
    )
    barrier = pltpu.get_barrier_semaphore()
    for partner in partners:
        pl.semaphore_signal(barrier, inc=1, device_id=partner, device_id_type=MESH)

    sends = []

    def s_part(slot, part):
        if part is None:
            return s_tiles.at[slot]
        start, size = ((0, HALF_S), (HALF_S, WIRE_S - HALF_S))[part]
        return s_tiles.at[slot, pl.ds(start, size)]

    def x_part(slot):
        return x_tiles.at[slot]

    def s_copy(source, target, device, part=None):
        copy = pltpu.make_async_remote_copy(
            src_ref=s_part(source, part), dst_ref=s_part(target, part),
            send_sem=sent.at[len(sends)], recv_sem=s_recv.at[target, part or 0],
            device_id=device, device_id_type=MESH,
        )
        sends.append(functools.partial(s_part, source, part))
        copy.start()

    def x_copy(source, target, device):
        copy = pltpu.make_async_remote_copy(
            src_ref=x_tiles.at[source], dst_ref=x_tiles.at[target],
            send_sem=sent.at[len(sends)], recv_sem=x_recv.at[target],
            device_id=device, device_id_type=MESH,
        )
        sends.append(functools.partial(x_part, source))
        copy.start()

    def s_wait(slot, part=None):
        ref = s_part(slot, part)
        pltpu.make_async_remote_copy(
            src_ref=ref, dst_ref=ref, send_sem=sent.at[0], recv_sem=s_recv.at[slot, part or 0],
            device_id=sibling, device_id_type=MESH,
        ).wait_recv()

    def x_wait(slot):
        ref = x_tiles.at[slot]
        pltpu.make_async_remote_copy(
            src_ref=ref, dst_ref=ref, send_sem=sent.at[0], recv_sem=x_recv.at[slot],
            device_id=sibling, device_id_type=MESH,
        ).wait_recv()

    lane = lax.broadcasted_iota(jnp.int32, (1, LANES), 1)
    unit = (
        lax.broadcasted_iota(jnp.int32, (BLOCK, BLOCK), 0)
        == lax.broadcasted_iota(jnp.int32, (BLOCK, BLOCK), 1)
    ).astype(jnp.bfloat16)

    def lane_columns(where, number, wide, slot):
        first = wide * LANES // BLOCK
        values = []
        for block in (first, first + 1):
            live = slot < number[block]
            values.append(jnp.where(live, where[block, slot], -1).astype(jnp.float32))
        return jnp.where(lane + wide * LANES < (first + 1) * BLOCK, values[0], values[1])

    meta[...] = jnp.full_like(meta, -1.0)
    for wide in range(WIDE_S):
        for slot in range(SLOTS_S):
            index = wide * SLOTS_S + slot
            meta[index : index + 1, :] = lane_columns(b_cols, b_count, wide, slot)
    s_tiles[0, DATA_S:, :] = meta[...].astype(jnp.bfloat16)
    for slot in range(SLOTS_S):
        turned = nt(unit, s_in[slot]).astype(jnp.bfloat16)
        for wide in range(WIDE_S):
            index = wide * SLOTS_S + slot
            s_tiles[0, index * BLOCK : (index + 1) * BLOCK, :] = turned[
                :, wide * LANES : (wide + 1) * LANES
            ]
    pl.semaphore_wait(barrier, len(partners))
    s_copy(0, s_slot(0, -1), along_y(1))
    s_copy(0, s_slot(0, 1), along_y(-1))

    meta[...] = jnp.full_like(meta, -1.0)
    for wide in range(WIDE_X):
        for slot in range(SLOTS_X):
            index = wide * SLOTS_X + slot
            meta[index : index + 1, :] = lane_columns(a_cols, a_count, wide, slot)
    x_tiles[0, DATA_X:, :] = meta[...].astype(jnp.bfloat16)
    for slot in range(SLOTS_X):
        turned = nt(unit, x_in[slot]).astype(jnp.bfloat16)
        for wide in range(WIDE_X):
            index = wide * SLOTS_X + slot
            x_tiles[0, index * BLOCK : (index + 1) * BLOCK, :] = turned[
                :, wide * LANES : (wide + 1) * LANES
            ]
    x_copy(0, x_slot(1, 0, 0), far_chip)
    for d in (1, -1, 2):
        x_copy(0, x_slot(0, -d, 0), along_x(d))
    x_copy(0, x_slot(0, 0, 1), sibling)
    s_copy(0, s_slot(1, 0), pair_chip)
    total[...] = jnp.zeros_like(total)

    def s_ring(other, near):
        for sign in (1, -1):
            here = s_slot(other, sign * near)
            s_wait(here)
            s_copy(here, s_slot(other, sign * (near + 1)), along_y(-sign))

    def x_share(other, dx):
        x_wait(x_slot(other, dx, 0))
        x_copy(x_slot(other, dx, 0), x_slot(other, dx, 1), sibling)

    def step_1():
        s_ring(0, 1)
        x_wait(x_slot(0, 0, 1))

    def step_2():
        x_share(0, 1)
        x_share(0, -1)

    def step_3():
        s_ring(0, 2)
        x_wait(x_slot(0, 1, 1))

    def step_4():
        here = x_slot(1, 0, 0)
        x_wait(here)
        for d in (1, -1, 2):
            x_copy(here, x_slot(1, -d, 0), along_x(d))
        x_copy(here, x_slot(1, 0, 1), sibling)

    def step_5():
        s_wait(s_slot(0, 3))
        s_copy(s_slot(0, 3), s_slot(0, 4), along_y(-1), 1)
        s_wait(s_slot(0, -3))
        s_copy(s_slot(0, -3), s_slot(0, 4), along_y(1), 0)
        s_wait(s_slot(1, 0))
        s_copy(s_slot(1, 0), s_slot(1, 1), along_y(-1))
        s_copy(s_slot(1, 0), s_slot(1, -1), along_y(1))
        for sign in (1, -1):
            s_copy(s_slot(0, sign * 3), s_slot(1, sign * 3), pair_chip, 0)
        x_wait(x_slot(0, -1, 1))

    def step_6():
        x_share(0, 2)

    def step_7():
        for part in (0, 1):
            s_wait(s_slot(0, 4), part)
        s_copy(s_slot(0, 4), s_slot(1, 4), pair_chip)
        x_wait(x_slot(0, 2, 1))

    def step_9():
        s_ring(1, 1)
        x_wait(x_slot(1, 0, 1))

    def step_10():
        x_share(1, 1)
        x_share(1, -1)

    def step_11():
        for sign in (1, -1):
            here = s_slot(1, sign * 2)
            s_wait(here)
            s_copy(here, s_slot(1, sign * 3), along_y(-sign), 1)
        x_wait(x_slot(1, 1, 1))

    def step_13():
        for sign in (1, -1):
            for part in (0, 1):
                s_wait(s_slot(1, sign * 3), part)
        x_wait(x_slot(1, -1, 1))

    def step_14():
        x_share(1, 2)

    def step_15():
        s_wait(s_slot(1, 4))
        x_wait(x_slot(1, 2, 1))

    events = {
        1: step_1, 2: step_2, 3: step_3, 4: step_4, 5: step_5, 6: step_6, 7: step_7, 9: step_9,
        10: step_10, 11: step_11, 13: step_13, 14: step_14, 15: step_15,
    }

    def x_for_s(s_at):
        h = s_at % 8
        dy = ((h + 1) // 2) * (2 * (h % 2) - 1)
        other = s_at // 8
        u = ((parity + other) % 2) * 8 + (y + dy + 8) % 8
        t = (u + col - row + 32) % 16
        dx = (t // 4 - x + 4) % 4
        place = jnp.where(dx == 3, 2, jnp.where(dx == 2, 3, dx))
        far = ((t // 2) % 2 + z_hi) % 2
        return far * 8 + place * 2 + (t % 2 + core) % 2

    def s_for_x(x_at):
        place = (x_at // 2) % 4
        dx = jnp.where(place == 3, 2, jnp.where(place == 2, 3, place))
        t = ((x + dx) % 4) * 4 + ((z_hi + x_at // 8) % 2) * 2 + (core + x_at) % 2
        u = (t + row - col + 16) % 16
        dy = (u % 8 - y + 8) % 8
        h = jnp.where(dy == 0, 0, jnp.where(dy <= 4, 2 * dy - 1, 2 * (8 - dy)))
        return ((u // 8 + parity) % 2) * 8 + h

    def multiply(s_at, x_at):
        names = x_tiles[x_at, DATA_X:, :]
        for wide in range(WIDE_X):
            stored, column = [], []
            for slot in range(SLOTS_X):
                index = wide * SLOTS_X + slot
                stored.append(x_tiles[x_at, index * BLOCK : (index + 1) * BLOCK, :])
                column.append(jnp.broadcast_to(names[index : index + 1, :], (BLOCK, LANES)))
            for j in range(COLS):
                placed = jnp.zeros((BLOCK, LANES), jnp.bfloat16)
                for slot in range(SLOTS_X):
                    placed = jnp.where(column[slot] == j, stored[slot], placed)
                x_dense[j * BLOCK : (j + 1) * BLOCK, wide * LANES : (wide + 1) * LANES] = placed
        names = s_tiles[s_at, DATA_S:, :]
        for wide in range(WIDE_S):
            stored, column = [], []
            for slot in range(SLOTS_S):
                index = wide * SLOTS_S + slot
                stored.append(s_tiles[s_at, index * BLOCK : (index + 1) * BLOCK, :])
                column.append(jnp.broadcast_to(names[index : index + 1, :], (BLOCK, LANES)))
            for j in range(COLS):
                placed = jnp.zeros((BLOCK, LANES), jnp.bfloat16)
                for slot in range(SLOTS_S):
                    placed = jnp.where(column[slot] == j, stored[slot], placed)
                s_dense[j * BLOCK : (j + 1) * BLOCK, wide * LANES : (wide + 1) * LANES] = placed
        total[...] += jnp.dot(s_dense[...], x_dense[...], preferred_element_type=jnp.float32)

        own = (s_at // 8 + parity) % 2 * 8
        h = s_at % 8
        dy = ((h + 1) // 2) * (2 * (h % 2) - 1)

        @pl.when(own + (y + dy + 8) % 8 == 0)
        def _():
            total[...] -= 3.0 * x_dense[...].astype(jnp.float32)

    def body(step, carry):
        place = step // 2
        by_x = step % 2
        for at_place, event in events.items():
            pl.when(step == 2 * at_place)(event)
        s_at = jnp.where(by_x == 1, s_for_x(place), place)
        x_at = jnp.where(by_x == 1, place, x_for_s(place))
        ready = jnp.where(by_x == 1, s_at < place, x_at <= place)

        @pl.when(ready)
        def _():
            multiply(s_at, x_at)

        return carry

    lax.fori_loop(0, 32, body, 0)
    out_ref[...] = (-0.5 * total[...]).astype(jnp.bfloat16)
    assert len(sends) == N_SENDS
    for index, part in enumerate(sends):
        pltpu.make_async_remote_copy(
            src_ref=part(), dst_ref=part(), send_sem=sent.at[index], recv_sem=x_recv.at[0],
            device_id=sibling, device_id_type=MESH,
        ).wait_send()


N_SENDS = 33


def shards(a_vals, a_cols, a_count, b_vals, b_cols, b_count):
    x_in = a_vals.reshape(ROWS, SLOTS_X, BLOCK, BLOCK).transpose(1, 0, 2, 3)
    x_in = x_in.reshape(SLOTS_X, ROWS * BLOCK, BLOCK)
    s_in = b_vals.reshape(COLS, SLOTS_S, BLOCK, BLOCK).transpose(1, 0, 2, 3)
    s_in = s_in.reshape(SLOTS_S, COLS * BLOCK, BLOCK)
    scalars = pl.BlockSpec(memory_space=pltpu.SMEM)
    blocks = pl.BlockSpec(memory_space=pltpu.VMEM)
    turned = pl.pallas_call(
        kernel,
        out_shape=jax.ShapeDtypeStruct((COLS * BLOCK, ROWS * BLOCK), jnp.bfloat16),
        in_specs=[scalars] * 4 + [blocks] * 2,
        out_specs=blocks,
        scratch_shapes=[
            pltpu.VMEM((16, WIRE_X, LANES), jnp.bfloat16),
            pltpu.VMEM((16, WIRE_S, LANES), jnp.bfloat16),
            pltpu.VMEM((COLS * BLOCK, ROWS * BLOCK), jnp.bfloat16),
            pltpu.VMEM((COLS * BLOCK, COLS * BLOCK), jnp.bfloat16),
            pltpu.VMEM((COLS * BLOCK, ROWS * BLOCK), jnp.float32),
            pltpu.VMEM((META, LANES), jnp.float32),
            pltpu.SemaphoreType.DMA((16,)),
            pltpu.SemaphoreType.DMA((16, 2)),
            pltpu.SemaphoreType.DMA((N_SENDS,)),
        ],
        compiler_params=pltpu.CompilerParams(
            collective_id=0, has_side_effects=True, vmem_limit_bytes=40 * 1024 * 1024
        ),
        name="gather_multiply",
    )(a_cols[0, 0], a_count[0, 0], b_cols[0, 0], b_count[0, 0], x_in, s_in)
    return turned.T


def solution(mesh):
    in_specs = (
        P("row", "col", None, None, None),
        P("row", "col", None, None),
        P("row", "col", None),
        P("row", "col", None, None, None),
        P("row", "col", None, None),
        P("row", "col", None),
    )
    out_specs = P("row", "col")
    return jax.shard_map(shards, mesh=mesh, in_specs=in_specs, out_specs=out_specs, check_vma=False)
```

time: 592 us -> 70.8 us (0.12); the launches traced: 583 us -> 69.8 us
  starting transfers between devices: 294 us -> 0 us
  local copies, waits for them, and re-layouts: 128 us -> 5.16 us
  waiting for transfers between devices: 67.1 us -> 0 us
  Pallas kernels: 0 us -> 64.6 us
  matrix products: 58.9 us -> 0 us
  other arithmetic: 31 us -> 0 us
    ppermute x90 -> x0, starting transfers between devices: 294 us -> none  [passed_along(): lax.ppermute(shard, axis, [(i, (i + by) % count) for i in range(count)])]
    ppermute x90 -> x0, waiting for transfers between devices: 67.1 us -> none  [passed_along(): lax.ppermute(shard, axis, [(i, (i + by) % count) for i in range(count)])]
    pallas_call x0 -> x1, Pallas kernels: none -> 64.6 us  [shards(): pl.pallas_call(kernel, out_shape=jax.ShapeDtypeStruct((COLS * BLOCK, ROWS...]
    dot_general x33 -> x0, matrix products: 58.9 us -> none  [the longest x16 44.5 us: tile_term(): jnp.einsum('ipxk,ipkn->ixn', blocks, picked_rows, preferred_element_type=...]
    gather x16 -> x0, local copies, waits for them, and re-layouts: 39.9 us -> none  [tile_term(): picked_rows = panel[a_where]]
    while x240 -> x0, local copies, waits for them, and re-layouts: 29.8 us -> none
    select_n x62 -> x0, other arithmetic: 29.5 us -> none  [the longest x45 28.3 us: advance(): jnp.where(shift_step == own_step, arrived, stored)]
    squeeze x30 -> x1, local copies, waits for them, and re-layouts: 22.7 us -> 0.08 us  [shards(): b_cols[0, 0]]
  transfers between devices with their start and end apart: 90 -> 0, of which waited for: 15 -> 0; matrix products, arithmetic and copies ran while one was open for 31% -> 0% of each run, Pallas kernels for 0% -> 0%
where the time goes in v1:
time: 70.8 us; the launch traced here: 69.8 us
  Pallas kernels  64.6 us (91%)
  local copies, waits for them, and re-layouts  5.16 us (7%)
    pallas_call x1, Pallas kernels, shards(): pl.pallas_call(kernel, out_shape=jax.ShapeDtypeStruct((COLS * BLOCK, ROWS...  64.6 us
    unnamed x10, local copies, waits for them, and re-layouts  2.28 us

profile of v1, /device:TPU:56, one launch (start us, length us, event | category | flops | bytes accessed | tf_op | source)
XLA Modules:
  0.0 69.8 jit_solution(7049773502268884192)
XLA Ops:
  0.0 0.0 copy-start.4
  0.0 0.7 copy-done.4
  0.7 0.1 copy.8.b_cols
  0.8 1.3 %reshape.14 = bf16[8,2,96,96]{3,2,1,0:T(8,128)(2,1)S(1)} reshape(bf16[1,1,8,2,9216]{4,3,2,1,0:T(2,128)(2,1)} %param.9) | data formatting | bytes 589824 | tf_op jit(solution)/shard_map/reshape | solution.py:334
  2.1 0.0 copy-start.3
  2.1 0.9 %copy-done.3 = bf16[1,1,4,5,9216]{4,2,3,1,0:T(4,128)(2,1)S(1)} copy-done((bf16[1,1,4,5,9216]{4,2,3,1,0:T(4,128)(2,1)S(1)}, bf16[1,1,4,5,9216]{4,2,3,1,0:T(4,128)(2,1)}, u32[]{:S(2)}) %copy-start.3) | copy-done | bytes 368664
  3.1 0.0 copy-start
  3.1 0.4 reshape.12
  3.5 0.0 copy-start.1
  3.5 0.0 copy-start.2
  3.5 0.3 copy-done
  3.7 0.4 copy-done.1
  4.1 0.0 copy-done.2
  4.1 64.6 %gather_multiply.1 = bf16[768,384]{1,0:T(8,128)(2,1)S(1)} custom-call(s32[4,5]{1,0:T(4,128)S(1)} %bitcast.16, s32[4]{0:T(128)S(1)} %bitcast.17, s32[8,2]{1,0:T(8,128)S(1)} %copy.8.b_cols, s32[8]{0:T(128)S(1)} %bitcast.18, bf16[5,384,96]{2,1,0:T(8,128)(2,1)S(1)} %bitcast.14, bf16[2,768,96]{2,1,0:T(8,128)(2,1)S(1)} %bitcast.15), custom_call_target="tpu_custom_call" | custom-call | tf_op jit(solution)/shard_map/gather_multiply/pallas_call | solution.py:338
  68.8 1.1 %copy.9 = bf16[384,768]{1,0:T(8,128)(2,1)} copy(bf16[384,768]{0,1:T(8,128)(2,1)S(1)} %bitcast.13) | data formatting | bytes 1179648 | tf_op jit(solution)/shard_map/transpose | solution.py:359
  (1 shorter events, 0.0 us)
Async XLA Ops:
  0.0 0.7 copy-start.4
  2.1 1.0 %copy-start.3 = (bf16[1,1,4,5,9216]{4,2,3,1,0:T(4,128)(2,1)S(1)}, bf16[1,1,4,5,9216]{4,2,3,1,0:T(4,128)(2,1)}, u32[]{:S(2)}) copy-start(bf16[1,1,4,5,9216]{4,2,3,1,0:T(4,128)(2,1)} %param.6) | copy-start | bytes 1105924
  3.1 0.7 copy-start
  3.5 0.7 copy-start.1
  3.5 0.7 copy-start.2

commit v2 on v1

v2 whole, which is shorter than its diff:
```python
import functools

import jax
import jax.numpy as jnp
from jax import lax
from jax.experimental import pallas as pl
from jax.experimental.pallas import tpu as pltpu
from jax.sharding import PartitionSpec as P

BLOCK = 96
LANES = 128
ROWS = 4
SLOTS_X = 5
COLS = 8
SLOTS_S = 2
WIDE_X = ROWS * BLOCK // LANES
WIDE_S = COLS * BLOCK // LANES
DATA_X = WIDE_X * SLOTS_X * BLOCK
DATA_S = WIDE_S * SLOTS_S * BLOCK
META = 16
WIRE_X = DATA_X + META
WIRE_S = DATA_S + META
SPLIT_X = (0, 720, WIRE_X)
SPLIT_S = (0, 576, WIRE_S)
MESH = pl.DeviceIdType.MESH
AROUND = (0, 1, 3, 2)
HALVES = (0, 1)
OWN = {0: 0, 1: 1, -1: 2, 2: 3, -2: 4, 3: 5, -3: 6, 4: 7}
OTHER = {0: 8, 1: 9, -1: 10, 2: 12, -2: 13, 4: 14}
BY_PAIR, BY_RING = 11, 15


def x_slot(other, dx, sibling=0):
    return 8 * other + 2 * AROUND.index(dx % 4) + sibling


def nt(left, right):
    return lax.dot_general(
        left, right, (((1,), (1,)), ((), ())), preferred_element_type=jnp.float32
    )


def kernel(
    a_cols, a_count, b_cols, b_count, x_in, s_in, out_ref,
    x_tiles, s_tiles, x_dense, s_dense, total, meta, x_recv, s_recv, sent,
):
    row, col = lax.axis_index("row"), lax.axis_index("col")
    y, z_lo = row % 8, row // 8
    core, z_hi, x = col % 2, (col // 2) % 2, col // 4
    parity = z_lo % 2

    def at(x_at, y_at, z_lo_at, z_hi_at, core_at):
        return (z_lo_at * 8 + y_at, (x_at * 2 + z_hi_at) * 2 + core_at)

    def along_x(d):
        return at((x + d + 4) % 4, y, z_lo, z_hi, core)

    def along_y(d):
        return at(x, (y + d + 8) % 8, z_lo, z_hi, core)

    pair_chip = at(x, y, z_lo + 1 - 2 * parity, z_hi, core)
    far_chip = at(x, y, z_lo, 1 - z_hi, core)
    sibling = at(x, y, z_lo, z_hi, 1 - core)
    near_chips = (along_x(1), along_x(-1), along_y(1), along_y(-1), pair_chip, sibling)
    barrier = pltpu.get_barrier_semaphore()

    def greet(device):
        pl.semaphore_signal(barrier, inc=1, device_id=device, device_id_type=MESH)

    for device in near_chips:
        greet(device)

    sends = []

    def s_part(slot, half):
        start = SPLIT_S[half]
        return s_tiles.at[slot, pl.ds(start, SPLIT_S[half + 1] - start)]

    def x_part(slot, half):
        start = SPLIT_X[half]
        return x_tiles.at[slot, pl.ds(start, SPLIT_X[half + 1] - start)]

    def send(part, arrived, source, target, device, half, index=None):
        if index is None:
            index = len(sends)
            sends.append(functools.partial(part, source, half))
        pltpu.make_async_remote_copy(
            src_ref=part(source, half), dst_ref=part(target, half),
            send_sem=sent.at[index], recv_sem=arrived.at[target, half],
            device_id=device, device_id_type=MESH,
        ).start()

    def wait(part, arrived, slot, half):
        ref = part(slot, half)
        pltpu.make_async_remote_copy(
            src_ref=ref, dst_ref=ref, send_sem=sent.at[0], recv_sem=arrived.at[slot, half],
            device_id=sibling, device_id_type=MESH,
        ).wait_recv()

    s_copy = functools.partial(send, s_part, s_recv)
    x_copy = functools.partial(send, x_part, x_recv)
    s_wait = functools.partial(wait, s_part, s_recv)
    x_wait = functools.partial(wait, x_part, x_recv)

    lane = lax.broadcasted_iota(jnp.int32, (1, LANES), 1)
    unit = (
        lax.broadcasted_iota(jnp.int32, (BLOCK, BLOCK), 0)
        == lax.broadcasted_iota(jnp.int32, (BLOCK, BLOCK), 1)
    ).astype(jnp.bfloat16)

    def lane_columns(where, number, wide, slot):
        first = wide * LANES // BLOCK
        values = []
        for block in (first, first + 1):
            live = slot < number[block]
            values.append(jnp.where(live, where[block, slot], -1).astype(jnp.float32))
        return jnp.where(lane + wide * LANES < (first + 1) * BLOCK, values[0], values[1])

    meta[...] = jnp.full_like(meta, -1.0)
    for wide in range(WIDE_S):
        for slot in range(SLOTS_S):
            index = wide * SLOTS_S + slot
            meta[index : index + 1, :] = lane_columns(b_cols, b_count, wide, slot)
    s_tiles[0, DATA_S:, :] = meta[...].astype(jnp.bfloat16)
    for slot in range(SLOTS_S):
        turned = nt(unit, s_in[slot]).astype(jnp.bfloat16)
        for wide in range(WIDE_S):
            index = wide * SLOTS_S + slot
            s_tiles[0, index * BLOCK : (index + 1) * BLOCK, :] = turned[
                :, wide * LANES : (wide + 1) * LANES
            ]
    pl.semaphore_wait(barrier, len(near_chips) + z_hi)
    greet(far_chip)
    for half in HALVES:
        s_copy(0, OWN[-1], along_y(1), half)
        s_copy(0, OWN[1], along_y(-1), half)

    meta[...] = jnp.full_like(meta, -1.0)
    for wide in range(WIDE_X):
        for slot in range(SLOTS_X):
            index = wide * SLOTS_X + slot
            meta[index : index + 1, :] = lane_columns(a_cols, a_count, wide, slot)
    x_tiles[0, DATA_X:, :] = meta[...].astype(jnp.bfloat16)
    for slot in range(SLOTS_X):
        turned = nt(unit, x_in[slot]).astype(jnp.bfloat16)
        for wide in range(WIDE_X):
            index = wide * SLOTS_X + slot
            x_tiles[0, index * BLOCK : (index + 1) * BLOCK, :] = turned[
                :, wide * LANES : (wide + 1) * LANES
            ]
    far_sends = len(sends)
    sends.extend(functools.partial(x_part, 0, half) for half in HALVES)

    def x_leave():
        for half in HALVES:
            x_copy(0, x_slot(1, 0), far_chip, half, far_sends + half)

    def x_leave_late():
        @pl.when(z_hi == 0)
        def _():
            pl.semaphore_wait(barrier, 1)
            x_leave()

    pl.when(z_hi == 1)(x_leave)
    for half in HALVES:
        x_copy(0, x_slot(0, -1), along_x(1), half)
        x_copy(0, x_slot(0, 1), along_x(-1), half)
    for half in HALVES:
        x_copy(0, x_slot(0, 0, 1), sibling, half)
    for half in HALVES:
        s_copy(0, OTHER[0], pair_chip, half)
    total[...] = jnp.zeros_like(total)

    def s_ring(slots, near, half):
        for sign in (1, -1):
            here = slots[sign * near]
            s_wait(here, half)
            s_copy(here, slots[sign * (near + 1)], along_y(-sign), half)

    def x_near(other):
        for half in HALVES:
            for d in (1, -1):
                here = x_slot(other, d)
                x_wait(here, half)
                if (half == 0) == (d == 1):
                    x_copy(here, x_slot(other, 2), along_x(-d), half)
                x_copy(here, here + 1, sibling, half)

    def x_across(other):
        here = x_slot(other, 2)
        for half in HALVES:
            x_wait(here, half)
            x_copy(here, here + 1, sibling, half)

    def x_far(half):
        here = x_slot(1, 0)
        x_wait(here, half)
        x_copy(here, x_slot(1, -1), along_x(1), half)
        x_copy(here, x_slot(1, 1), along_x(-1), half)
        x_copy(here, here + 1, sibling, half)

    def x_sibling(other, dx):
        for half in HALVES:
            x_wait(x_slot(other, dx, 1), half)

    pair_third = OWN[-3] - core
    ring_second, other_second = OTHER[2] + core, OTHER[-2] - core
    ring_chip = along_y(2 * core - 1)

    def s_third_first():
        s_wait(OWN[3], 0)
        s_copy(OWN[3], OWN[4], along_y(-1), 0)
        s_wait(OWN[-3], 0)
        s_copy(pair_third, BY_PAIR, pair_chip, 0)

    def s_third_last():
        s_wait(OWN[-3], 1)
        s_copy(OWN[-3], OWN[4], along_y(1), 1)
        s_wait(OWN[3], 1)
        s_copy(pair_third, BY_PAIR, pair_chip, 1)

    def s_other_start():
        for half in HALVES:
            s_wait(OTHER[0], half)
            s_copy(OTHER[0], OTHER[1], along_y(-1), half)
            s_copy(OTHER[0], OTHER[-1], along_y(1), half)

    def s_fourth():
        for half in HALVES:
            s_wait(OWN[4], half)
            s_copy(OWN[4], OTHER[4], pair_chip, half)

    def s_other_second():
        for half in HALVES:
            s_wait(ring_second, half)
            s_copy(ring_second, BY_RING, ring_chip, half)
        for half in HALVES:
            s_wait(other_second, half)

    def s_last(slot):
        for half in HALVES:
            s_wait(slot, half)

    part = functools.partial
    plan = (
        "S", "X",
        part(s_ring, OWN, 1, 0), part(x_sibling, 0, 0), "X",
        part(s_ring, OWN, 1, 1), x_leave_late, "S", "S",
        part(s_ring, OWN, 2, 0), part(x_far, 0), part(x_near, 0), "X",
        part(s_ring, OWN, 2, 1), "S", "S",
        part(x_sibling, 0, 1), "X", "X", part(x_sibling, 0, -1), "X",
        s_third_first, part(x_far, 1), s_third_last, "S", "S",
        s_other_start, part(x_across, 0), "X", part(x_sibling, 0, 2), "X",
        s_fourth, "S", "S",
        "X", part(x_sibling, 1, 0), "X",
        part(s_ring, OTHER, 1, 0), part(x_near, 1), "X", part(x_sibling, 1, 1), "X",
        part(s_ring, OTHER, 1, 1), "S", "S",
        "X", part(x_sibling, 1, -1), "X", part(x_across, 1), "X", part(x_sibling, 1, 2), "X",
        part(s_last, BY_PAIR), "S",
        s_other_second, "S", "S",
        part(s_last, OTHER[4]), "S",
        part(s_last, BY_RING), "S",
    )
    events, turns, bits = {}, 0, 0
    for entry in plan:
        if entry in ("S", "X"):
            bits += (entry == "X") << turns
            turns += 1
        else:
            events.setdefault(turns, []).append(entry)
    low_bits, high_bits = bits % 2**16, bits // 2**16
    third = 3 - 6 * core

    def distance(s_at):
        h = s_at % 8
        own = ((h + 1) // 2) * (2 * (h % 2) - 1)
        tail = jnp.where(h == 3, -third, jnp.where(h == 7, third, jnp.where(h == 6, 4, 18 - 4 * h)))
        return jnp.where((s_at >= 8) & (h >= 3), tail, own)

    def s_row(s_at):
        return (parity + s_at // 8) % 2 * 8 + (y + distance(s_at) + 8) % 8

    def x_for_s(s_at):
        t = (s_row(s_at) + col - row + 32) % 16
        dx = (t // 4 - x + 4) % 4
        place = jnp.where(dx == 3, 2, jnp.where(dx == 2, 3, dx))
        far = ((t // 2) % 2 + z_hi) % 2
        return far * 8 + place * 2 + (t % 2 + core) % 2

    def s_for_x(x_at):
        place = (x_at // 2) % 4
        dx = jnp.where(place == 3, 2, jnp.where(place == 2, 3, place))
        t = ((x + dx) % 4) * 4 + ((z_hi + x_at // 8) % 2) * 2 + (core + x_at) % 2
        u = (t + row - col + 16) % 16
        dy = (u % 8 - y + 8) % 8
        dy = jnp.where(dy > 4, dy - 8, dy)
        own = jnp.where(dy > 0, 2 * dy - 1, -2 * dy)
        tail = jnp.where(dy == third, 7, jnp.where(dy == -third, 3, jnp.where(dy == 4, 6, own + 1)))
        tail = jnp.where(own < 3, own, tail)
        return jnp.where((u // 8 + parity) % 2 == 1, 8 + tail, own)

    def multiply(s_at, x_at):
        names = x_tiles[x_at, DATA_X:, :]
        for wide in range(WIDE_X):
            stored, column = [], []
            for slot in range(SLOTS_X):
                index = wide * SLOTS_X + slot
                stored.append(x_tiles[x_at, index * BLOCK : (index + 1) * BLOCK, :])
                column.append(jnp.broadcast_to(names[index : index + 1, :], (BLOCK, LANES)))
            for j in range(COLS):
                placed = jnp.zeros((BLOCK, LANES), jnp.bfloat16)
                for slot in range(SLOTS_X):
                    placed = jnp.where(column[slot] == j, stored[slot], placed)
                x_dense[j * BLOCK : (j + 1) * BLOCK, wide * LANES : (wide + 1) * LANES] = placed
        names = s_tiles[s_at, DATA_S:, :]
        for wide in range(WIDE_S):
            stored, column = [], []
            for slot in range(SLOTS_S):
                index = wide * SLOTS_S + slot
                stored.append(s_tiles[s_at, index * BLOCK : (index + 1) * BLOCK, :])
                column.append(jnp.broadcast_to(names[index : index + 1, :], (BLOCK, LANES)))
            for j in range(COLS):
                placed = jnp.zeros((BLOCK, LANES), jnp.bfloat16)
                for slot in range(SLOTS_S):
                    placed = jnp.where(column[slot] == j, stored[slot], placed)
                s_dense[j * BLOCK : (j + 1) * BLOCK, wide * LANES : (wide + 1) * LANES] = placed
        total[...] += jnp.dot(s_dense[...], x_dense[...], preferred_element_type=jnp.float32)

        @pl.when(s_row(s_at) == 0)
        def _():
            total[...] -= 3.0 * x_dense[...].astype(jnp.float32)

    def body(step, arrived):
        s_count, x_count = arrived
        for turn, entries in events.items():

            @pl.when(step == turn)
            def _():
                for entry in entries:
                    entry()

        by_x = (jnp.where(step < 16, low_bits, high_bits) >> (step % 16)) % 2
        s_at = jnp.where(by_x == 1, s_for_x(x_count), s_count)
        x_at = jnp.where(by_x == 1, x_count, x_for_s(s_count))
        ready = jnp.where(by_x == 1, s_at < s_count, x_at < x_count)

        @pl.when(ready)
        def _():
            multiply(s_at, x_at)

        return s_count + 1 - by_x, x_count + by_x

    lax.fori_loop(0, turns, body, (0, 0))
    out_ref[...] = (-0.5 * total[...]).astype(jnp.bfloat16)
    assert len(sends) == N_SENDS, len(sends)
    for index, ref in enumerate(sends):
        pltpu.make_async_remote_copy(
            src_ref=ref(), dst_ref=ref(), send_sem=sent.at[index], recv_sem=x_recv.at[0, 0],
            device_id=sibling, device_id_type=MESH,
        ).wait_send()


N_SENDS = 60


def shards(a_vals, a_cols, a_count, b_vals, b_cols, b_count):
    x_in = a_vals.reshape(ROWS, SLOTS_X, BLOCK, BLOCK).transpose(1, 0, 2, 3)
    x_in = x_in.reshape(SLOTS_X, ROWS * BLOCK, BLOCK)
    s_in = b_vals.reshape(COLS, SLOTS_S, BLOCK, BLOCK).transpose(1, 0, 2, 3)
    s_in = s_in.reshape(SLOTS_S, COLS * BLOCK, BLOCK)
    scalars = pl.BlockSpec(memory_space=pltpu.SMEM)
    blocks = pl.BlockSpec(memory_space=pltpu.VMEM)
    turned = pl.pallas_call(
        kernel,
        out_shape=jax.ShapeDtypeStruct((COLS * BLOCK, ROWS * BLOCK), jnp.bfloat16),
        in_specs=[scalars] * 4 + [blocks] * 2,
        out_specs=blocks,
        scratch_shapes=[
            pltpu.VMEM((16, WIRE_X, LANES), jnp.bfloat16),
            pltpu.VMEM((16, WIRE_S, LANES), jnp.bfloat16),
            pltpu.VMEM((COLS * BLOCK, ROWS * BLOCK), jnp.bfloat16),
            pltpu.VMEM((COLS * BLOCK, COLS * BLOCK), jnp.bfloat16),
            pltpu.VMEM((COLS * BLOCK, ROWS * BLOCK), jnp.float32),
            pltpu.VMEM((META, LANES), jnp.float32),
            pltpu.SemaphoreType.DMA((16, 2)),
            pltpu.SemaphoreType.DMA((16, 2)),
            pltpu.SemaphoreType.DMA((N_SENDS,)),
        ],
        compiler_params=pltpu.CompilerParams(
            collective_id=0, has_side_effects=True, vmem_limit_bytes=40 * 1024 * 1024
        ),
        name="gather_multiply",
    )(a_cols[0, 0], a_count[0, 0], b_cols[0, 0], b_count[0, 0], x_in, s_in)
    return turned.T


def solution(mesh):
    in_specs = (
        P("row", "col", None, None, None),
        P("row", "col", None, None),
        P("row", "col", None),
        P("row", "col", None, None, None),
        P("row", "col", None, None),
        P("row", "col", None),
    )
    out_specs = P("row", "col")
    return jax.shard_map(shards, mesh=mesh, in_specs=in_specs, out_specs=out_specs, check_vma=False)
```

time: 70.8 us -> 67.3 us (0.951)
  the two profiles are of different devices: /device:TPU:56 before, /device:TPU:137 now
where the time goes in v2:
time: 67.3 us; the launch traced here: 67.1 us
  Pallas kernels  61.9 us (92%)
  local copies, waits for them, and re-layouts  5.16 us (8%)
    pallas_call x1, Pallas kernels, shards(): pl.pallas_call(kernel, out_shape=jax.ShapeDtypeStruct((COLS * BLOCK, ROWS...  61.9 us
    unnamed x10, local copies, waits for them, and re-layouts  2.28 us

profile of v2, /device:TPU:137, one launch (start us, length us, event | category | flops | bytes accessed | tf_op | source)
XLA Modules:
  0.0 67.1 jit_solution(17446081141624928482)
XLA Ops:
  0.0 0.0 copy-start.4
  0.0 0.7 %copy-done.4 = s32[1,1,8,2]{2,3,1,0:T(2,128)S(1)} copy-done((s32[1,1,8,2]{2,3,1,0:T(2,128)S(1)}, s32[1,1,8,2]{2,3,1,0:T(2,128)}, u32[]{:S(2)}) %copy-start.4) | copy-done | bytes 88
  0.7 0.1 copy.8.b_cols
  0.8 1.3 %reshape.14 = bf16[8,2,96,96]{3,2,1,0:T(8,128)(2,1)S(1)} reshape(bf16[1,1,8,2,9216]{4,3,2,1,0:T(2,128)(2,1)} %param.9) | data formatting | bytes 589824 | tf_op jit(solution)/shard_map/reshape | solution.py:369
  2.1 0.0 copy-start.3
  2.1 0.9 %copy-done.3 = bf16[1,1,4,5,9216]{4,2,3,1,0:T(4,128)(2,1)S(1)} copy-done((bf16[1,1,4,5,9216]{4,2,3,1,0:T(4,128)(2,1)S(1)}, bf16[1,1,4,5,9216]{4,2,3,1,0:T(4,128)(2,1)}, u32[]{:S(2)}) %copy-start.3) | copy-done | bytes 368664
  3.1 0.0 copy-start
  3.1 0.4 reshape.12
  3.5 0.0 copy-start.1
  3.5 0.0 copy-start.2
  3.5 0.3 copy-done
  3.7 0.4 copy-done.1
  4.1 0.0 copy-done.2
  4.1 61.9 %gather_multiply.1 = bf16[768,384]{1,0:T(8,128)(2,1)S(1)} custom-call(s32[4,5]{1,0:T(4,128)S(1)} %bitcast.16, s32[4]{0:T(128)S(1)} %bitcast.17, s32[8,2]{1,0:T(8,128)S(1)} %copy.8.b_cols, s32[8]{0:T(128)S(1)} %bitcast.18, bf16[5,384,96]{2,1,0:T(8,128)(2,1)S(1)} %bitcast.14, bf16[2,768,96]{2,1,0:T(8,128)(2,1)S(1)} %bitcast.15), custom_call_target="tpu_custom_call" | custom-call | tf_op jit(solution)/shard_map/gather_multiply/pallas_call | solution.py:373
  66.0 1.1 %copy.9 = bf16[384,768]{1,0:T(8,128)(2,1)} copy(bf16[384,768]{0,1:T(8,128)(2,1)S(1)} %bitcast.13) | data formatting | bytes 1179648 | tf_op jit(solution)/shard_map/transpose | solution.py:394
  (1 shorter events, 0.0 us)
Async XLA Ops:
  0.0 0.7 %copy-start.4 = (s32[1,1,8,2]{2,3,1,0:T(2,128)S(1)}, s32[1,1,8,2]{2,3,1,0:T(2,128)}, u32[]{:S(2)}) copy-start(s32[1,1,8,2]{2,3,1,0:T(2,128)} %param.10) | copy-start | bytes 196
  2.1 1.0 %copy-start.3 = (bf16[1,1,4,5,9216]{4,2,3,1,0:T(4,128)(2,1)S(1)}, bf16[1,1,4,5,9216]{4,2,3,1,0:T(4,128)(2,1)}, u32[]{:S(2)}) copy-start(bf16[1,1,4,5,9216]{4,2,3,1,0:T(4,128)(2,1)} %param.6) | copy-start | bytes 1105924
  3.1 0.7 %copy-start = (s32[1,1,4,5]{3,2,1,0:T(4,128)S(1)}, s32[1,1,4,5]{3,2,1,0:T(4,128)}, u32[]{:S(2)}) copy-start(s32[1,1,4,5]{3,2,1,0:T(4,128)} %param.7) | copy-start | bytes 244
  3.5 0.7 copy-start.1
  3.5 0.7 copy-start.2

commit v3 on v2

--- a/solution.py
+++ b/solution.py
@@ -34,6 +34,14 @@
     return 8 * other + 2 * AROUND.index(dx % 4) + sibling
 
 
+def div(number, by):
+    return lax.div(number, jnp.int32(by))
+
+
+def rem(number, by):
+    return lax.rem(number, jnp.int32(by))
+
+
 def nt(left, right):
     return lax.dot_general(
         left, right, (((1,), (1,)), ((), ())), preferred_element_type=jnp.float32
@@ -41,22 +49,22 @@
 
 
 def kernel(
-    a_cols, a_count, b_cols, b_count, x_in, s_in, out_ref,
-    x_tiles, s_tiles, x_dense, s_dense, total, meta, x_recv, s_recv, sent,
+    a_cols_in, a_count_in, b_cols_in, b_count_in, x_in, s_in, out_ref,
+    a_cols, a_count, b_cols, b_count, scalars_came, x_tiles, s_tiles, x_dense, s_dense, total, meta, x_recv, s_recv, sent,
 ):
     row, col = lax.axis_index("row"), lax.axis_index("col")
-    y, z_lo = row % 8, row // 8
-    core, z_hi, x = col % 2, (col // 2) % 2, col // 4
-    parity = z_lo % 2
+    y, z_lo = rem(row, 8), div(row, 8)
+    core, z_hi, x = rem(col, 2), rem(div(col, 2), 2), div(col, 4)
+    parity = rem(z_lo, 2)
 
     def at(x_at, y_at, z_lo_at, z_hi_at, core_at):
         return (z_lo_at * 8 + y_at, (x_at * 2 + z_hi_at) * 2 + core_at)
 
     def along_x(d):
-        return at((x + d + 4) % 4, y, z_lo, z_hi, core)
+        return at(rem(x + d + 4, 4), y, z_lo, z_hi, core)
 
     def along_y(d):
-        return at(x, (y + d + 8) % 8, z_lo, z_hi, core)
+        return at(x, rem(y + d + 8, 8), z_lo, z_hi, core)
 
     pair_chip = at(x, y, z_lo + 1 - 2 * parity, z_hi, core)
     far_chip = at(x, y, z_lo, 1 - z_hi, core)
@@ -69,6 +77,14 @@
 
     for device in near_chips:
         greet(device)
+    scalars = [
+        pltpu.make_async_copy(source, target, scalars_came.at[index])
+        for index, (source, target) in enumerate(
+            ((a_cols_in, a_cols), (a_count_in, a_count), (b_cols_in, b_cols), (b_count_in, b_count))
+        )
+    ]
+    for copy in scalars:
+        copy.start()
 
     sends = []
 
@@ -113,14 +129,16 @@
         values = []
         for block in (first, first + 1):
             live = slot < number[block]
-            values.append(jnp.where(live, where[block, slot], -1).astype(jnp.float32))
+            values.append(jnp.where(live, where(block, slot), -1).astype(jnp.float32))
         return jnp.where(lane + wide * LANES < (first + 1) * BLOCK, values[0], values[1])
 
+    for copy in scalars:
+        copy.wait()
     meta[...] = jnp.full_like(meta, -1.0)
     for wide in range(WIDE_S):
         for slot in range(SLOTS_S):
             index = wide * SLOTS_S + slot
-            meta[index : index + 1, :] = lane_columns(b_cols, b_count, wide, slot)
+            meta[index : index + 1, :] = lane_columns(lambda block, slot: b_cols[slot, block], b_count, wide, slot)
     s_tiles[0, DATA_S:, :] = meta[...].astype(jnp.bfloat16)
     for slot in range(SLOTS_S):
         turned = nt(unit, s_in[slot]).astype(jnp.bfloat16)
@@ -139,7 +157,7 @@
     for wide in range(WIDE_X):
         for slot in range(SLOTS_X):
             index = wide * SLOTS_X + slot
-            meta[index : index + 1, :] = lane_columns(a_cols, a_count, wide, slot)
+            meta[index : index + 1, :] = lane_columns(lambda block, slot: a_cols[block, slot], a_count, wide, slot)
     x_tiles[0, DATA_X:, :] = meta[...].astype(jnp.bfloat16)
     for slot in range(SLOTS_X):
         turned = nt(unit, x_in[slot]).astype(jnp.bfloat16)
@@ -177,14 +195,13 @@
             s_wait(here, half)
             s_copy(here, slots[sign * (near + 1)], along_y(-sign), half)
 
-    def x_near(other):
-        for half in HALVES:
-            for d in (1, -1):
-                here = x_slot(other, d)
-                x_wait(here, half)
-                if (half == 0) == (d == 1):
-                    x_copy(here, x_slot(other, 2), along_x(-d), half)
-                x_copy(here, here + 1, sibling, half)
+    def x_near(other, half):
+        for d in (1, -1):
+            here = x_slot(other, d)
+            x_wait(here, half)
+            if (half == 0) == (d == 1):
+                x_copy(here, x_slot(other, 2), along_x(-d), half)
+            x_copy(here, here + 1, sibling, half)
 
     def x_across(other):
         here = x_slot(other, 2)
@@ -230,12 +247,9 @@
             s_wait(OWN[4], half)
             s_copy(OWN[4], OTHER[4], pair_chip, half)
 
-    def s_other_second():
-        for half in HALVES:
-            s_wait(ring_second, half)
-            s_copy(ring_second, BY_RING, ring_chip, half)
-        for half in HALVES:
-            s_wait(other_second, half)
+    def s_other_second(half):
+        s_wait(ring_second, half)
+        s_copy(ring_second, BY_RING, ring_chip, half)
 
     def s_last(slot):
         for half in HALVES:
@@ -246,19 +260,19 @@
         "S", "X",
         part(s_ring, OWN, 1, 0), part(x_sibling, 0, 0), "X",
         part(s_ring, OWN, 1, 1), x_leave_late, "S", "S",
-        part(s_ring, OWN, 2, 0), part(x_far, 0), part(x_near, 0), "X",
+        part(s_ring, OWN, 2, 0), part(x_near, 0, 0), part(x_near, 0, 1), "X",
         part(s_ring, OWN, 2, 1), "S", "S",
-        part(x_sibling, 0, 1), "X", "X", part(x_sibling, 0, -1), "X",
-        s_third_first, part(x_far, 1), s_third_last, "S", "S",
-        s_other_start, part(x_across, 0), "X", part(x_sibling, 0, 2), "X",
-        s_fourth, "S", "S",
-        "X", part(x_sibling, 1, 0), "X",
-        part(s_ring, OTHER, 1, 0), part(x_near, 1), "X", part(x_sibling, 1, 1), "X",
-        part(s_ring, OTHER, 1, 1), "S", "S",
-        "X", part(x_sibling, 1, -1), "X", part(x_across, 1), "X", part(x_sibling, 1, 2), "X",
-        part(s_last, BY_PAIR), "S",
-        s_other_second, "S", "S",
+        part(x_sibling, 0, 1), "X", "X",
+        s_third_first, part(x_sibling, 0, -1), "X", part(x_across, 0), s_third_last, part(x_far, 0), "S", "S",
+        s_other_start, "X", part(x_sibling, 0, 2), "X",
+        s_fourth, part(x_far, 1), "S", "S",
+        "X", part(s_ring, OTHER, 1, 0), part(x_near, 1, 0), part(x_sibling, 1, 0), "X",
+        part(s_ring, OTHER, 1, 1), part(x_near, 1, 1), "S", "S", "X",
+        part(s_other_second, 0), part(x_sibling, 1, 1), "X", "X", part(s_last, BY_PAIR), "S",
+        part(s_other_second, 1), part(x_sibling, 1, -1), "X", part(x_across, 1),
+        part(s_last, other_second), "S", "S", "X",
         part(s_last, OTHER[4]), "S",
+        part(x_sibling, 1, 2), "X",
         part(s_last, BY_RING), "S",
     )
     events, turns, bits = {}, 0, 0
@@ -272,32 +286,32 @@
     third = 3 - 6 * core
 
     def distance(s_at):
-        h = s_at % 8
-        own = ((h + 1) // 2) * (2 * (h % 2) - 1)
+        h = rem(s_at, 8)
+        own = div(h + 1, 2) * (2 * rem(h, 2) - 1)
         tail = jnp.where(h == 3, -third, jnp.where(h == 7, third, jnp.where(h == 6, 4, 18 - 4 * h)))
         return jnp.where((s_at >= 8) & (h >= 3), tail, own)
 
     def s_row(s_at):
-        return (parity + s_at // 8) % 2 * 8 + (y + distance(s_at) + 8) % 8
+        return rem(parity + div(s_at, 8), 2) * 8 + rem(y + distance(s_at) + 8, 8)
 
     def x_for_s(s_at):
-        t = (s_row(s_at) + col - row + 32) % 16
-        dx = (t // 4 - x + 4) % 4
+        t = rem(s_row(s_at) + col - row + 32, 16)
+        dx = rem(div(t, 4) - x + 4, 4)
         place = jnp.where(dx == 3, 2, jnp.where(dx == 2, 3, dx))
-        far = ((t // 2) % 2 + z_hi) % 2
-        return far * 8 + place * 2 + (t % 2 + core) % 2
+        far = rem(div(t, 2) + z_hi, 2)
+        return far * 8 + place * 2 + rem(t + core, 2)
 
     def s_for_x(x_at):
-        place = (x_at // 2) % 4
+        place = rem(div(x_at, 2), 4)
         dx = jnp.where(place == 3, 2, jnp.where(place == 2, 3, place))
-        t = ((x + dx) % 4) * 4 + ((z_hi + x_at // 8) % 2) * 2 + (core + x_at) % 2
-        u = (t + row - col + 16) % 16
-        dy = (u % 8 - y + 8) % 8
+        t = rem(x + dx, 4) * 4 + rem(z_hi + div(x_at, 8), 2) * 2 + rem(core + x_at, 2)
+        u = rem(t + row - col + 16, 16)
+        dy = rem(u - y + 8, 8)
         dy = jnp.where(dy > 4, dy - 8, dy)
         own = jnp.where(dy > 0, 2 * dy - 1, -2 * dy)
         tail = jnp.where(dy == third, 7, jnp.where(dy == -third, 3, jnp.where(dy == 4, 6, own + 1)))
         tail = jnp.where(own < 3, own, tail)
-        return jnp.where((u // 8 + parity) % 2 == 1, 8 + tail, own)
+        return jnp.where(rem(div(u, 8) + parity, 2) == 1, 8 + tail, own)
 
     def multiply(s_at, x_at):
         names = x_tiles[x_at, DATA_X:, :]
@@ -330,16 +344,22 @@
         def _():
             total[...] -= 3.0 * x_dense[...].astype(jnp.float32)
 
+    def happen(step, first, last):
+        if last - first == 1:
+            for entry in events.get(first, ()):
+                entry()
+        elif any(first <= turn < last for turn in events):
+            middle = (first + last) // 2
+            lax.cond(
+                step < middle,
+                lambda: happen(step, first, middle),
+                lambda: happen(step, middle, last),
+            )
+
     def body(step, arrived):
         s_count, x_count = arrived
-        for turn, entries in events.items():
-
-            @pl.when(step == turn)
-            def _():
-                for entry in entries:
-                    entry()
-
-        by_x = (jnp.where(step < 16, low_bits, high_bits) >> (step % 16)) % 2
+        happen(step, 0, turns)
+        by_x = (jnp.where(step < 16, low_bits, high_bits) >> rem(step, 16)) & 1
         s_at = jnp.where(by_x == 1, s_for_x(x_count), s_count)
         x_at = jnp.where(by_x == 1, x_count, x_for_s(s_count))
         ready = jnp.where(by_x == 1, s_at < s_count, x_at < x_count)
@@ -350,7 +370,7 @@
 
         return s_count + 1 - by_x, x_count + by_x
 
-    lax.fori_loop(0, turns, body, (0, 0))
+    lax.fori_loop(0, turns, body, (jnp.int32(0), jnp.int32(0)))
     out_ref[...] = (-0.5 * total[...]).astype(jnp.bfloat16)
     assert len(sends) == N_SENDS, len(sends)
     for index, ref in enumerate(sends):
@@ -368,14 +388,18 @@
     x_in = x_in.reshape(SLOTS_X, ROWS * BLOCK, BLOCK)
     s_in = b_vals.reshape(COLS, SLOTS_S, BLOCK, BLOCK).transpose(1, 0, 2, 3)
     s_in = s_in.reshape(SLOTS_S, COLS * BLOCK, BLOCK)
-    scalars = pl.BlockSpec(memory_space=pltpu.SMEM)
     blocks = pl.BlockSpec(memory_space=pltpu.VMEM)
     turned = pl.pallas_call(
         kernel,
         out_shape=jax.ShapeDtypeStruct((COLS * BLOCK, ROWS * BLOCK), jnp.bfloat16),
-        in_specs=[scalars] * 4 + [blocks] * 2,
+        in_specs=[pl.BlockSpec(memory_space=pl.ANY)] * 4 + [blocks] * 2,
         out_specs=blocks,
         scratch_shapes=[
+            pltpu.SMEM((ROWS, SLOTS_X), jnp.int32),
+            pltpu.SMEM((ROWS,), jnp.int32),
+            pltpu.SMEM((SLOTS_S, COLS), jnp.int32),
+            pltpu.SMEM((COLS,), jnp.int32),
+            pltpu.SemaphoreType.DMA((4,)),
             pltpu.VMEM((16, WIRE_X, LANES), jnp.bfloat16),
             pltpu.VMEM((16, WIRE_S, LANES), jnp.bfloat16),
             pltpu.VMEM((COLS * BLOCK, ROWS * BLOCK), jnp.bfloat16),
@@ -390,7 +414,7 @@
             collective_id=0, has_side_effects=True, vmem_limit_bytes=40 * 1024 * 1024
         ),
         name="gather_multiply",
-    )(a_cols[0, 0], a_count[0, 0], b_cols[0, 0], b_count[0, 0], x_in, s_in)
+    )(a_cols[0, 0], a_count[0, 0], b_cols[0, 0].T, b_count[0, 0], x_in, s_in)
     return turned.T
 
 

time: 67.3 us -> 57.7 us (0.86)
  the two profiles are of different devices: /device:TPU:137 before, /device:TPU:56 now
where the time goes in v3:
time: 57.7 us; the launch traced here: 56.7 us
  Pallas kernels  52.2 us (90%)
  local copies, waits for them, and re-layouts  4.41 us (8%)
    pallas_call x1, Pallas kernels, shards(): pl.pallas_call(kernel, out_shape=jax.ShapeDtypeStruct((COLS * BLOCK, ROWS...  52.2 us
    unnamed x10, local copies, waits for them, and re-layouts  1.62 us
    reshape x2, local copies, waits for them, and re-layouts, shards(): s_in = b_vals.reshape(COLS, SLOTS_S, BLOCK, BLOCK).transpose(1, 0, 2, 3)  1.33 us

profile of v3, /device:TPU:56, one launch (start us, length us, event | category | flops | bytes accessed | tf_op | source)
XLA Modules:
  0.0 56.7 jit_solution(3131975865768896031)
XLA Ops:
  0.0 1.3 %reshape.14 = bf16[8,2,96,96]{3,2,1,0:T(8,128)(2,1)S(1)} reshape(bf16[1,1,8,2,9216]{4,3,2,1,0:T(2,128)(2,1)} %param.9) | data formatting | bytes 589824 | tf_op jit(solution)/shard_map/reshape | solution.py:389
  1.3 0.0 copy-start.4
  1.4 0.9 %copy-done.4 = bf16[1,1,4,5,9216]{4,2,3,1,0:T(4,128)(2,1)S(1)} copy-done((bf16[1,1,4,5,9216]{4,2,3,1,0:T(4,128)(2,1)S(1)}, bf16[1,1,4,5,9216]{4,2,3,1,0:T(4,128)(2,1)}, u32[]{:S(2)}) %copy-start.4) | copy-done | bytes 368664
  2.3 0.0 copy-start
  2.3 0.0 copy-start.3
  2.3 0.4 reshape.12
  2.7 0.0 copy-start.1
  2.7 0.0 copy-start.2
  2.7 0.3 copy-done
  3.0 0.0 copy-done.3
  3.0 0.4 copy-done.1
  3.4 0.0 copy-done.2
  3.4 52.2 %gather_multiply.1 = bf16[768,384]{1,0:T(8,128)(2,1)S(1)} custom-call(s32[4,5]{1,0:T(4,128)S(1)} %bitcast.18, s32[4]{0:T(128)S(1)} %bitcast.20, s32[2,8]{1,0:T(2,128)S(1)} %bitcast.19, s32[8]{0:T(128)S(1)} %bitcast.21, bf16[5,384,96]{2,1,0:T(8,128)(2,1)S(1)} %bitcast.16, bf16[2,768,96]{2,1,0:T(8,128)(2,1)S(1)} %bitcast.17), custom_call_target="tpu_custom_call" | custom-call | tf_op jit(solution)/shard_map/gather_multiply/pallas_call | solution.py:392
  55.6 1.1 %copy.8 = bf16[384,768]{1,0:T(8,128)(2,1)} copy(bf16[384,768]{0,1:T(8,128)(2,1)S(1)} %bitcast.15) | data formatting | bytes 1179648 | tf_op jit(solution)/shard_map/transpose | solution.py:418
  (1 shorter events, 0.0 us)
Async XLA Ops:
  1.3 1.0 %copy-start.4 = (bf16[1,1,4,5,9216]{4,2,3,1,0:T(4,128)(2,1)S(1)}, bf16[1,1,4,5,9216]{4,2,3,1,0:T(4,128)(2,1)}, u32[]{:S(2)}) copy-start(bf16[1,1,4,5,9216]{4,2,3,1,0:T(4,128)(2,1)} %param.6) | copy-start | bytes 1105924
  2.3 0.7 %copy-start = (s32[1,1,4,5]{3,2,1,0:T(4,128)S(1)}, s32[1,1,4,5]{3,2,1,0:T(4,128)}, u32[]{:S(2)}) copy-start(s32[1,1,4,5]{3,2,1,0:T(4,128)} %param.7) | copy-start | bytes 244
  2.3 0.7 %copy-start.3 = (s32[1,1,8]{2,1,0:T(1,128)S(1)}, s32[1,1,8]{2,1,0:T(1,128)}, u32[]{:S(2)}) copy-start(s32[1,1,8]{2,1,0:T(1,128)} %param.11) | copy-start | bytes 100
  2.7 0.7 %copy-start.1 = (s32[1,1,8,2]{2,3,1,0:T(2,128)S(1)}, s32[1,1,8,2]{2,3,1,0:T(2,128)}, u32[]{:S(2)}) copy-start(s32[1,1,8,2]{2,3,1,0:T(2,128)} %param.10) | copy-start | bytes 196
  2.7 0.7 %copy-start.2 = (s32[1,1,4]{2,1,0:T(1,128)S(1)}, s32[1,1,4]{2,1,0:T(1,128)}, u32[]{:S(2)}) copy-start(s32[1,1,4]{2,1,0:T(1,128)} %param.8) | copy-start | bytes 52

commit v4 on v3

--- a/solution.py
+++ b/solution.py
@@ -255,24 +255,36 @@
         for half in HALVES:
             s_wait(slot, half)
 
+    left = [0]
+
+    def sends_leave(end):
+        for index in range(left[0], end):
+            ref = sends[index]()
+            pltpu.make_async_remote_copy(
+                src_ref=ref, dst_ref=ref, send_sem=sent.at[index], recv_sem=x_recv.at[0, 0],
+                device_id=sibling, device_id_type=MESH,
+            ).wait_send()
+        left[0] = end
+
     part = functools.partial
     plan = (
         "S", "X",
-        part(s_ring, OWN, 1, 0), part(x_sibling, 0, 0), "X",
-        part(s_ring, OWN, 1, 1), x_leave_late, "S", "S",
+        part(s_ring, OWN, 1, 0), x_leave_late, part(x_sibling, 0, 0), "X",
+        part(s_ring, OWN, 1, 1), "S", "S",
         part(s_ring, OWN, 2, 0), part(x_near, 0, 0), part(x_near, 0, 1), "X",
         part(s_ring, OWN, 2, 1), "S", "S",
         part(x_sibling, 0, 1), "X", "X",
         s_third_first, part(x_sibling, 0, -1), "X", part(x_across, 0), s_third_last, part(x_far, 0), "S", "S",
         s_other_start, "X", part(x_sibling, 0, 2), "X",
-        s_fourth, part(x_far, 1), "S", "S",
+        s_fourth, part(x_far, 1), part(sends_leave, 20), "S", "S",
         "X", part(s_ring, OTHER, 1, 0), part(x_near, 1, 0), part(x_sibling, 1, 0), "X",
         part(s_ring, OTHER, 1, 1), part(x_near, 1, 1), "S", "S", "X",
         part(s_other_second, 0), part(x_sibling, 1, 1), "X", "X", part(s_last, BY_PAIR), "S",
-        part(s_other_second, 1), part(x_sibling, 1, -1), "X", part(x_across, 1),
-        part(s_last, other_second), "S", "S", "X",
+        part(x_sibling, 1, -1), "X", part(x_across, 1), "X",
+        part(s_other_second, 1), part(sends_leave, 40),
+        part(s_last, other_second), "S", "S",
+        part(x_sibling, 1, 2), "X",
         part(s_last, OTHER[4]), "S",
-        part(x_sibling, 1, 2), "X",
         part(s_last, BY_RING), "S",
     )
     events, turns, bits = {}, 0, 0
@@ -373,11 +385,7 @@
     lax.fori_loop(0, turns, body, (jnp.int32(0), jnp.int32(0)))
     out_ref[...] = (-0.5 * total[...]).astype(jnp.bfloat16)
     assert len(sends) == N_SENDS, len(sends)
-    for index, ref in enumerate(sends):
-        pltpu.make_async_remote_copy(
-            src_ref=ref(), dst_ref=ref(), send_sem=sent.at[index], recv_sem=x_recv.at[0, 0],
-            device_id=sibling, device_id_type=MESH,
-        ).wait_send()
+    sends_leave(len(sends))
 
 
 N_SENDS = 60
@@ -386,6 +394,7 @@
 def shards(a_vals, a_cols, a_count, b_vals, b_cols, b_count):
     x_in = a_vals.reshape(ROWS, SLOTS_X, BLOCK, BLOCK).transpose(1, 0, 2, 3)
     x_in = x_in.reshape(SLOTS_X, ROWS * BLOCK, BLOCK)
+    b_vals, x_in = lax.optimization_barrier((b_vals, x_in))
     s_in = b_vals.reshape(COLS, SLOTS_S, BLOCK, BLOCK).transpose(1, 0, 2, 3)
     s_in = s_in.reshape(SLOTS_S, COLS * BLOCK, BLOCK)
     blocks = pl.BlockSpec(memory_space=pltpu.VMEM)
@@ -414,7 +423,14 @@
             collective_id=0, has_side_effects=True, vmem_limit_bytes=40 * 1024 * 1024
         ),
         name="gather_multiply",
-    )(a_cols[0, 0], a_count[0, 0], b_cols[0, 0].T, b_count[0, 0], x_in, s_in)
+    )(
+        *(
+            pltpu.with_memory_space_constraint(number, pltpu.HBM)
+            for number in (a_cols[0, 0], a_count[0, 0], b_cols[0, 0].T, b_count[0, 0])
+        ),
+        x_in,
+        s_in,
+    )
     return turned.T
 
 

time: 57.7 us -> 55.5 us (0.962); the launches traced: 56.7 us -> 55.4 us
  local copies, waits for them, and re-layouts: 4.41 us -> 2.88 us
    unnamed x10 -> x2, local copies, waits for them, and re-layouts: 1.62 us -> 0.01 us
    reshape x1, local copies, waits for them, and re-layouts: 0.39 us -> 1.44 us  [shards(): x_in = a_vals.reshape(ROWS, SLOTS_X, BLOCK, BLOCK).transpose(1, 0, 2, 3)]
    reshape x2, local copies, waits for them, and re-layouts: 1.33 us -> 0.36 us  [shards(): s_in = b_vals.reshape(COLS, SLOTS_S, BLOCK, BLOCK).transpose(1, 0, 2, 3)]
where the time goes in v4:
time: 55.5 us; the launch traced here: 55.4 us
  Pallas kernels  52.4 us (94%)
  local copies, waits for them, and re-layouts  2.88 us (5%)
    pallas_call x1, Pallas kernels, shards(): pl.pallas_call(kernel, out_shape=jax.ShapeDtypeStruct((COLS * BLOCK, ROWS...  52.4 us
    reshape x1, local copies, waits for them, and re-layouts, shards(): x_in = a_vals.reshape(ROWS, SLOTS_X, BLOCK, BLOCK).transpose(1, 0, 2, 3)  1.44 us

profile of v4, /device:TPU:56, one launch (start us, length us, event | category | flops | bytes accessed | tf_op | source)
XLA Modules:
  0.0 55.4 jit_solution(8586453871849446715)
XLA Ops:
  0.0 0.0 copy-start
  0.0 1.4 %reshape.12 = bf16[4,5,96,96]{3,2,0,1:T(8,128)(2,1)S(1)} reshape(bf16[1,1,4,5,9216]{4,2,3,1,0:T(4,128)(2,1)} %param.6) | data formatting | bytes 737280 | tf_op jit(solution)/shard_map/reshape | solution.py:395
  1.4 0.0 copy-done
  1.5 0.3 reshape.14
  1.8 52.4 %gather_multiply.1 = bf16[768,384]{1,0:T(8,128)(2,1)S(1)} custom-call(s32[4,5]{1,0:T(4,128)} %bitcast.18, s32[4]{0:T(128)} %bitcast.20, s32[2,8]{1,0:T(2,128)} %bitcast.19, s32[8]{0:T(128)} %bitcast.21, bf16[5,384,96]{2,1,0:T(8,128)(2,1)S(1)} %bitcast.16, bf16[2,768,96]{2,1,0:T(8,128)(2,1)S(1)} %bitcast.17), custom_call_target="tpu_custom_call" | custom-call | tf_op jit(solution)/shard_map/gather_multiply/pallas_call | solution.py:401
  54.3 1.1 %copy.8 = bf16[384,768]{1,0:T(8,128)(2,1)} copy(bf16[384,768]{0,1:T(8,128)(2,1)S(1)} %bitcast.15) | data formatting | bytes 1179648 | tf_op jit(solution)/shard_map/transpose | solution.py:434
  (1 shorter events, 0.0 us)
Async XLA Ops:
  0.0 1.5 %copy-start = (bf16[1,1,8,2,9216]{4,3,2,1,0:T(2,128)(2,1)S(1)}, bf16[1,1,8,2,9216]{4,3,2,1,0:T(2,128)(2,1)}, u32[]{:S(2)}) copy-start(bf16[1,1,8,2,9216]{4,3,2,1,0:T(2,128)(2,1)} %param.9) | copy-start | bytes 884740

commit v5 on v4

--- a/solution.py
+++ b/solution.py
@@ -132,14 +132,6 @@
             values.append(jnp.where(live, where(block, slot), -1).astype(jnp.float32))
         return jnp.where(lane + wide * LANES < (first + 1) * BLOCK, values[0], values[1])
 
-    for copy in scalars:
-        copy.wait()
-    meta[...] = jnp.full_like(meta, -1.0)
-    for wide in range(WIDE_S):
-        for slot in range(SLOTS_S):
-            index = wide * SLOTS_S + slot
-            meta[index : index + 1, :] = lane_columns(lambda block, slot: b_cols[slot, block], b_count, wide, slot)
-    s_tiles[0, DATA_S:, :] = meta[...].astype(jnp.bfloat16)
     for slot in range(SLOTS_S):
         turned = nt(unit, s_in[slot]).astype(jnp.bfloat16)
         for wide in range(WIDE_S):
@@ -149,16 +141,24 @@
             ]
     pl.semaphore_wait(barrier, len(near_chips) + z_hi)
     greet(far_chip)
-    for half in HALVES:
+
+    def s_start(half):
         s_copy(0, OWN[-1], along_y(1), half)
         s_copy(0, OWN[1], along_y(-1), half)
 
+    s_start(0)
+    for copy in scalars:
+        copy.wait()
     meta[...] = jnp.full_like(meta, -1.0)
-    for wide in range(WIDE_X):
-        for slot in range(SLOTS_X):
-            index = wide * SLOTS_X + slot
-            meta[index : index + 1, :] = lane_columns(lambda block, slot: a_cols[block, slot], a_count, wide, slot)
-    x_tiles[0, DATA_X:, :] = meta[...].astype(jnp.bfloat16)
+    for wide in range(WIDE_S):
+        for slot in range(SLOTS_S):
+            index = wide * SLOTS_S + slot
+            meta[index : index + 1, :] = lane_columns(
+                lambda block, slot: b_cols[slot, block], b_count, wide, slot
+            )
+    s_tiles[0, DATA_S:, :] = meta[...].astype(jnp.bfloat16)
+    s_start(1)
+
     for slot in range(SLOTS_X):
         turned = nt(unit, x_in[slot]).astype(jnp.bfloat16)
         for wide in range(WIDE_X):
@@ -166,23 +166,32 @@
             x_tiles[0, index * BLOCK : (index + 1) * BLOCK, :] = turned[
                 :, wide * LANES : (wide + 1) * LANES
             ]
-    far_sends = len(sends)
-    sends.extend(functools.partial(x_part, 0, half) for half in HALVES)
-
-    def x_leave():
-        for half in HALVES:
-            x_copy(0, x_slot(1, 0), far_chip, half, far_sends + half)
+
+    def x_leave(half):
+        x_copy(0, x_slot(1, 0), far_chip, half, N_SENDS - 2 + half)
 
     def x_leave_late():
         @pl.when(z_hi == 0)
         def _():
             pl.semaphore_wait(barrier, 1)
-            x_leave()
-
-    pl.when(z_hi == 1)(x_leave)
-    for half in HALVES:
+            for half in HALVES:
+                x_leave(half)
+
+    def x_start(half):
+        pl.when(z_hi == 1)(functools.partial(x_leave, half))
         x_copy(0, x_slot(0, -1), along_x(1), half)
         x_copy(0, x_slot(0, 1), along_x(-1), half)
+
+    x_start(0)
+    meta[...] = jnp.full_like(meta, -1.0)
+    for wide in range(WIDE_X):
+        for slot in range(SLOTS_X):
+            index = wide * SLOTS_X + slot
+            meta[index : index + 1, :] = lane_columns(
+                lambda block, slot: a_cols[block, slot], a_count, wide, slot
+            )
+    x_tiles[0, DATA_X:, :] = meta[...].astype(jnp.bfloat16)
+    x_start(1)
     for half in HALVES:
         x_copy(0, x_slot(0, 0, 1), sibling, half)
     for half in HALVES:
@@ -384,8 +393,9 @@
 
     lax.fori_loop(0, turns, body, (jnp.int32(0), jnp.int32(0)))
     out_ref[...] = (-0.5 * total[...]).astype(jnp.bfloat16)
+    sends.extend(functools.partial(x_part, 0, half) for half in HALVES)
     assert len(sends) == N_SENDS, len(sends)
-    sends_leave(len(sends))
+    sends_leave(N_SENDS)
 
 
 N_SENDS = 60

time: 55.5 us -> 55.3 us (level); the launches traced: 55.4 us -> 54.3 us
  Pallas kernels: 52.4 us -> 51.4 us
    pallas_call x1, Pallas kernels: 52.4 us -> 51.4 us  [shards(): pl.pallas_call(kernel, out_shape=jax.ShapeDtypeStruct((COLS * BLOCK, ROWS...]
where the time goes in v5:
time: 55.3 us; the launch traced here: 54.3 us
  Pallas kernels  51.4 us (93%)
  local copies, waits for them, and re-layouts  2.88 us (5%)
    pallas_call x1, Pallas kernels, shards(): pl.pallas_call(kernel, out_shape=jax.ShapeDtypeStruct((COLS * BLOCK, ROWS...  51.4 us
    reshape x1, local copies, waits for them, and re-layouts, shards(): x_in = a_vals.reshape(ROWS, SLOTS_X, BLOCK, BLOCK).transpose(1, 0, 2, 3)  1.44 us

profile of v5, /device:TPU:56, one launch (start us, length us, event | category | flops | bytes accessed | tf_op | source)
XLA Modules:
  0.0 54.3 jit_solution(17121487215474707187)
XLA Ops:
  0.0 0.0 copy-start
  0.0 1.4 %reshape.12 = bf16[4,5,96,96]{3,2,0,1:T(8,128)(2,1)S(1)} reshape(bf16[1,1,4,5,9216]{4,2,3,1,0:T(4,128)(2,1)} %param.6) | data formatting | bytes 737280 | tf_op jit(solution)/shard_map/reshape | solution.py:405
  1.4 0.0 copy-done
  1.5 0.3 reshape.14
  1.8 51.4 %gather_multiply.1 = bf16[768,384]{1,0:T(8,128)(2,1)S(1)} custom-call(s32[4,5]{1,0:T(4,128)} %bitcast.18, s32[4]{0:T(128)} %bitcast.20, s32[2,8]{1,0:T(2,128)} %bitcast.19, s32[8]{0:T(128)} %bitcast.21, bf16[5,384,96]{2,1,0:T(8,128)(2,1)S(1)} %bitcast.16, bf16[2,768,96]{2,1,0:T(8,128)(2,1)S(1)} %bitcast.17), custom_call_target="tpu_custom_call" | custom-call | tf_op jit(solution)/shard_map/gather_multiply/pallas_call | solution.py:411
  53.2 1.1 %copy.8 = bf16[384,768]{1,0:T(8,128)(2,1)} copy(bf16[384,768]{0,1:T(8,128)(2,1)S(1)} %bitcast.15) | data formatting | bytes 1179648 | tf_op jit(solution)/shard_map/transpose | solution.py:444
  (1 shorter events, 0.0 us)
Async XLA Ops:
  0.0 1.5 %copy-start = (bf16[1,1,8,2,9216]{4,3,2,1,0:T(2,128)(2,1)S(1)}, bf16[1,1,8,2,9216]{4,3,2,1,0:T(2,128)(2,1)}, u32[]{:S(2)}) copy-start(bf16[1,1,8,2,9216]{4,3,2,1,0:T(2,128)(2,1)} %param.9) | copy-start | bytes 884740

commit v6 on v5

--- a/solution.py
+++ b/solution.py
@@ -21,7 +21,7 @@
 WIRE_X = DATA_X + META
 WIRE_S = DATA_S + META
 SPLIT_X = (0, 720, WIRE_X)
-SPLIT_S = (0, 576, WIRE_S)
+SPLIT_S = (0, 672, WIRE_S)
 MESH = pl.DeviceIdType.MESH
 AROUND = (0, 1, 3, 2)
 HALVES = (0, 1)
@@ -159,6 +159,12 @@
     s_tiles[0, DATA_S:, :] = meta[...].astype(jnp.bfloat16)
     s_start(1)
 
+    def s_pair():
+        for half in HALVES:
+            s_copy(0, OTHER[0], pair_chip, half, N_SENDS - 4 + half)
+
+    pl.when(z_hi == 0)(s_pair)
+
     for slot in range(SLOTS_X):
         turned = nt(unit, x_in[slot]).astype(jnp.bfloat16)
         for wide in range(WIDE_X):
@@ -194,8 +200,7 @@
     x_start(1)
     for half in HALVES:
         x_copy(0, x_slot(0, 0, 1), sibling, half)
-    for half in HALVES:
-        s_copy(0, OTHER[0], pair_chip, half)
+    pl.when(z_hi == 1)(s_pair)
     total[...] = jnp.zeros_like(total)
 
     def s_ring(slots, near, half):
@@ -393,6 +398,7 @@
 
     lax.fori_loop(0, turns, body, (jnp.int32(0), jnp.int32(0)))
     out_ref[...] = (-0.5 * total[...]).astype(jnp.bfloat16)
+    sends.extend(functools.partial(s_part, 0, half) for half in HALVES)
     sends.extend(functools.partial(x_part, 0, half) for half in HALVES)
     assert len(sends) == N_SENDS, len(sends)
     sends_leave(N_SENDS)

time: 55.3 us -> 55.5 us (level); the launches traced: 54.3 us -> 55.3 us
  Pallas kernels: 51.4 us -> 52.4 us
    pallas_call x1, Pallas kernels: 51.4 us -> 52.4 us  [shards(): pl.pallas_call(kernel, out_shape=jax.ShapeDtypeStruct((COLS * BLOCK, ROWS...]
where the time goes in v6:
time: 55.5 us; the launch traced here: 55.3 us
  Pallas kernels  52.4 us (94%)
  local copies, waits for them, and re-layouts  2.88 us (5%)
    pallas_call x1, Pallas kernels, shards(): pl.pallas_call(kernel, out_shape=jax.ShapeDtypeStruct((COLS * BLOCK, ROWS...  52.4 us
    reshape x1, local copies, waits for them, and re-layouts, shards(): x_in = a_vals.reshape(ROWS, SLOTS_X, BLOCK, BLOCK).transpose(1, 0, 2, 3)  1.44 us

profile of v6, /device:TPU:56, one launch (start us, length us, event | category | flops | bytes accessed | tf_op | source)
XLA Modules:
  0.0 55.3 jit_solution(623587359484101431)
XLA Ops:
  0.0 0.0 copy-start
  0.0 1.4 %reshape.12 = bf16[4,5,96,96]{3,2,0,1:T(8,128)(2,1)S(1)} reshape(bf16[1,1,4,5,9216]{4,2,3,1,0:T(4,128)(2,1)} %param.6) | data formatting | bytes 737280 | tf_op jit(solution)/shard_map/reshape | solution.py:411
  1.4 0.0 copy-done
  1.5 0.3 reshape.14
  1.8 52.4 %gather_multiply.1 = bf16[768,384]{1,0:T(8,128)(2,1)S(1)} custom-call(s32[4,5]{1,0:T(4,128)} %bitcast.18, s32[4]{0:T(128)} %bitcast.20, s32[2,8]{1,0:T(2,128)} %bitcast.19, s32[8]{0:T(128)} %bitcast.21, bf16[5,384,96]{2,1,0:T(8,128)(2,1)S(1)} %bitcast.16, bf16[2,768,96]{2,1,0:T(8,128)(2,1)S(1)} %bitcast.17), custom_call_target="tpu_custom_call" | custom-call | tf_op jit(solution)/shard_map/gather_multiply/pallas_call | solution.py:417
  54.2 1.1 %copy.8 = bf16[384,768]{1,0:T(8,128)(2,1)} copy(bf16[384,768]{0,1:T(8,128)(2,1)S(1)} %bitcast.15) | data formatting | bytes 1179648 | tf_op jit(solution)/shard_map/transpose | solution.py:450
  (1 shorter events, 0.0 us)
Async XLA Ops:
  0.0 1.5 %copy-start = (bf16[1,1,8,2,9216]{4,3,2,1,0:T(2,128)(2,1)S(1)}, bf16[1,1,8,2,9216]{4,3,2,1,0:T(2,128)(2,1)}, u32[]{:S(2)}) copy-start(bf16[1,1,8,2,9216]{4,3,2,1,0:T(2,128)(2,1)} %param.9) | copy-start | bytes 884740
